TPU v7x, 256 devices: a whole 4x4x8 slice. The times are simulated.
256 devices in a mesh: opt: 2 (over z_hi), dp: 8 (over x, core), tensor: 16 (over z_lo, y).
Axes of the slice: x: 4, y: 4, z: 8 (z_hi: 2, z_lo: 4; z = z_hi * 4 + z_lo), core: 2. Of those that a mesh axis runs over, the one named last changes fastest.
Arguments:
- tokens: bfloat16 [4096, 4096], P(('opt', 'dp')), may hold values from -6 to 6
- grad_hidden: bfloat16 [4096, 14336], P(('opt', 'dp'), 'tensor'), may hold values from -6 to 6
- weight_codes: bfloat16 [32, 128, 28672], P(('opt', 'dp'), None, 'tensor'), may hold values from -96 to 96
- scales: float32 [32, 224], P(('opt', 'dp'), 'tensor'), may hold values from 0.00048828125 to 0.001953125
- master: float32 [4096, 28672], P(('opt', 'dp'), 'tensor'), may hold values from -0.09375 to 0.09375
- first_moment: bfloat16 [4096, 28672], P(('opt', 'dp'), 'tensor'), may hold values from -6 to 6
- second_moment: bfloat16 [4096, 28672], P(('opt', 'dp'), 'tensor'), may hold values from 0.049804688 to 2
Outputs:
- hidden: bfloat16 [4096, 14336], P(('opt', 'dp'), 'tensor')
- grad_tokens: bfloat16 [4096, 4096], P(('opt', 'dp'), 'tensor')
- new_master: float32 [4096, 28672], P(('opt', 'dp'), 'tensor')
- new_first: bfloat16 [4096, 28672], P(('opt', 'dp'), 'tensor')
- new_second: bfloat16 [4096, 28672], P(('opt', 'dp'), 'tensor')
All inputs are finite; a program needn't handle non-finite values.
Results may differ from a plain program's by a relative error of at most 0.04.
Values may be sent and summed in bfloat16 or wider, within the bound.
No kernel may reach another device: no remote copies, remote signals or barrier semaphores. Data moves between devices by JAX's collectives and lax.ppermute only.
A program may use at most 192 MiB of HBM per device.

v0:
```python
import math

import jax
import jax.numpy as jnp
from jax import lax
from jax.sharding import PartitionSpec as P


def dequantize(weight_codes, scales):
    blocks, inner_rows, columns = weight_codes.shape
    scaled = (
        weight_codes.astype(jnp.float32).reshape(
            blocks, inner_rows, columns // inner_rows, inner_rows
        )
        * scales[:, None, :, None]
    )
    return scaled.reshape(blocks * inner_rows, columns).astype(jnp.bfloat16)


def adam_update(grads, master, first_moment, second_moment):
    adam_count = 20.0
    moment_one = 0.9 * first_moment.astype(jnp.float32) + 0.1 * grads
    moment_two = 0.95 * second_moment.astype(jnp.float32) + 0.05 * grads * grads
    fix_one = 1.0 - 0.9**adam_count
    fix_two = 1.0 - 0.95**adam_count
    direction = moment_one / fix_one / (jnp.sqrt(moment_two / fix_two) + 1e-08)
    new_master = master - 0.001 * (direction + 0.1 * master)
    return (new_master, moment_one.astype(jnp.bfloat16), moment_two.astype(jnp.bfloat16))


def project_all(tokens, full_codes, full_scales):
    weights = dequantize(full_codes, full_scales)
    projected = jnp.dot(tokens, weights, preferred_element_type=jnp.float32)
    return (weights, projected)


def body(tokens, grad_hidden, weight_codes, scales, master, first_moment, second_moment):
    tok_rows = tokens.shape[0]
    hidden_cols = weight_codes.shape[2]
    full_codes, full_scales = (
        lax.all_gather(weight_codes, ("opt", "dp"), axis=0, tiled=True),
        lax.all_gather(scales.astype(jnp.bfloat16), ("opt", "dp"), axis=0, tiled=True).astype(
            scales.dtype
        ),
    )
    weights, projected = project_all(tokens, full_codes, full_scales)
    half_cols = hidden_cols // 2
    gate_part = projected[:, :half_cols]
    up_part = projected[:, half_cols:]
    sigmoid_gate = jax.nn.sigmoid(gate_part)
    activated = gate_part * sigmoid_gate
    hidden = (activated * up_part).astype(jnp.bfloat16)
    upstream = grad_hidden.astype(jnp.float32)
    grad_gate = upstream * up_part * sigmoid_gate * (1.0 + gate_part * (1.0 - sigmoid_gate))
    grad_up = upstream * activated
    grad_proj = jnp.concatenate([grad_gate, grad_up], axis=1).astype(jnp.bfloat16)
    partial_tokens = lax.dot_general(
        grad_proj, weights, (((1,), (1,)), ((), ())), preferred_element_type=jnp.float32
    )
    grad_tokens = lax.psum_scatter(
        partial_tokens.astype(jnp.bfloat16), "tensor", scatter_dimension=1, tiled=True
    )
    grad_scale = 1.0 / math.sqrt(tok_rows * lax.axis_size(("opt", "dp")))
    product = lax.dot_general(
        tokens, grad_proj, (((0,), (0,)), ((), ())), preferred_element_type=jnp.float32
    )
    grads = lax.psum_scatter(
        (product * grad_scale).astype(jnp.bfloat16), ("opt", "dp"), scatter_dimension=0, tiled=True
    ).astype(jnp.float32)
    new_master, new_first, new_second = adam_update(grads, master, first_moment, second_moment)
    return (hidden, grad_tokens, new_master, new_first, new_second)


def solution(mesh):
    in_specs = (
        P(("opt", "dp"), None),
        P(("opt", "dp"), "tensor"),
        P(("opt", "dp"), None, "tensor"),
        P(("opt", "dp"), "tensor"),
        P(("opt", "dp"), "tensor"),
        P(("opt", "dp"), "tensor"),
        P(("opt", "dp"), "tensor"),
    )
    out_specs = (
        P(("opt", "dp"), "tensor"),
        P(("opt", "dp"), "tensor"),
        P(("opt", "dp"), "tensor"),
        P(("opt", "dp"), "tensor"),
        P(("opt", "dp"), "tensor"),
    )
    return jax.shard_map(body, mesh=mesh, in_specs=in_specs, out_specs=out_specs, check_vma=False)
```

profile of v0, /device:TPU:14, one launch (start us, length us, event | category | flops | bytes accessed | tf_op | source)
XLA Modules:
  0.0 556.1 jit_solution(16351507138838534267)
XLA Ops:
  7.2 0.0 copy-start
  7.2 0.0 all-gather.3.cloned.1.call-start
  7.2 0.7 all-gather.3.cloned.1.call-update
  7.9 0.0 reduce-scatter.5.cloned.1.call-start
  8.0 0.7 convert_bitcast_fusion
  8.6 24.7 %all-gather = bf16[16,2,14]{2,1,0:T(2,128)(2,1)S(1)} all-gather(bf16[1,2,14]{2,1,0:T(2,128)(2,1)S(1)} %convert_bitcast_fusion), channel_id=1, replica_groups=mesh['opt'=2,'dp'=8,'tensor'=16] {'opt','dp'}, dimensions={0}, use_global_device_ids=true | all-gather | bytes 952 | tf_op jit(solution)/shard_map/all_gather | solution.py:42
  33.3 0.1 copy.33
  33.4 1.2 copy.34
  34.7 135.0 %all-gather.3.cloned.1.call-done = bf16[32,128,1792]{2,1,0:T(8,128)(2,1)} async-done(((bf16[2,128,1792]{2,1,0:T(8,128)(2,1)}), bf16[32,128,1792]{2,1,0:T(8,128)(2,1)}) %all-gather.3.cloned.1.call-update) | async-done | bytes 14680080 | tf_op jit(solution)/shard_map/all_gather | solution.py:41
  169.7 16.5 %bitcast_convert_fusion = f32[4096,1792]{1,0:T(8,128)} fusion(bf16[32,128,1792]{2,1,0:T(8,128)(2,1)} %all-gather.3.cloned.1.call-done), kind=kLoop, calls=%fused_computation.3 | loop fusion | flops 7340032 | bytes 44040192 | tf_op jit(solution)/shard_map/reshape | solution.py:12
  186.2 29.5 %copy.43 = f32[4096,1792]{0,1:T(8,128)} copy(f32[4096,1792]{1,0:T(8,128)} %bitcast_convert_fusion) | data formatting | bytes 58720256 | tf_op jit(solution)/shard_map/reshape | solution.py:12
  215.7 13.5 %mul.72 = f32[32,128,14,128]{1,0,3,2:T(8,128)} broadcast(f32[32,14]{0,1:T(8,128)S(1)} %copy.33), dimensions={0,2} | broadcast | bytes 29361920 | tf_op jit(solution)/shard_map/mul | solution.py:12
  229.2 30.6 %fusion = bf16[4096,1792]{0,1:T(8,128)(2,1)} fusion(f32[4096,1792]{0,1:T(8,128)} %copy.43, f32[224,8,32,128]{3,2,1,0:T(8,128)} %bitcast.23), kind=kLoop, calls=%fused_computation.1 | loop fusion | flops 14680064 | bytes 73400320 | tf_op jit(solution)/shard_map/convert_element_type | solution.py:17
  259.8 0.0 copy-done
  259.8 7.3 %convolution_bitcast_fusion = f32[256,1792]{0,1:T(8,128)S(1)} fusion(bf16[4096,1792]{0,1:T(8,128)(2,1)} %fusion, bf16[256,4096]{1,0:T(8,128)(2,1)S(1)} %copy-done), kind=kOutput, calls=%fused_computation.7 | convolution fusion | flops 3758096384 | bytes 18612224 | tf_op jit(solution)/shard_map/dot_general | solution.py:33
  267.1 0.6 fusion.8
  267.8 0.0 copy-start.2
  267.8 0.8 copy-done.2
  268.5 8.3 %fusion.1 = bf16[4096,1792]{0,1:T(8,128)(2,1)} fusion(bf16[256,4096]{1,0:T(8,128)(2,1)S(1)} %copy-done, bf16[256,896]{0,1:T(8,128)(2,1)S(1)} %get-tuple-element.21, bf16[256,896]{0,1:T(8,128)(2,1)S(1)} %get-tuple-element.20), kind=kOutput, calls=%fused_computation.4 | convolution fusion | flops 3774611456 | bytes 17694720 | tf_op jit(solution)/shard_map/dot_general | solution.py:64
  276.8 0.0 copy-start.3
  276.8 0.0 reduce-scatter.5.cloned.1.call-update
  276.9 0.2 reduce-scatter.3.cloned.1.call-start
  277.1 0.8 copy-done.3
  277.8 10.4 %convolution_convert_fusion = bf16[256,4096]{1,0:T(8,128)(2,1)} fusion(bf16[4096,1792]{0,1:T(8,128)(2,1)} %fusion, bf16[256,896]{0,1:T(8,128)(2,1)S(1)} %copy-done.3, bf16[256,896]{0,1:T(8,128)(2,1)S(1)} %get-tuple-element.20), kind=kOutput, calls=%fused_computation.5 | convolution fusion | flops 3760979968 | bytes 17694720 | tf_op jit(solution)/shard_map/dot_general | solution.py:57
  288.2 0.0 reduce-scatter.3.cloned.1.call-update
  288.2 3.0 copy.38
  291.2 1.6 copy.35
  292.8 2.3 copy.36
  295.1 1.0 copy.39
  296.0 170.8 %reduce-scatter.5.cloned.1.call-done = bf16[256,1792]{0,1:T(8,128)(2,1)} async-done(((bf16[4096,1792]{0,1:T(8,128)(2,1)}), bf16[256,1792]{0,1:T(8,128)(2,1)}) %reduce-scatter.5.cloned.1.call-update) | async-done | bytes 917520 | tf_op jit(solution)/shard_map/reduce_scatter | solution.py:67
  466.8 6.0 %fusion.5 = (bf16[256,1792]{0,1:T(8,128)(2,1)}, f32[256,1792]{0,1:T(8,128)}, bf16[256,1792]{0,1:T(8,128)(2,1)}) fusion(bf16[256,1792]{0,1:T(8,128)(2,1)} %reduce-scatter.5.cloned.1.call-done, bf16[256,1792]{0,1:T(8,128)(2,1)} %copy.36, f32[256,1792]{0,1:T(8,128)} %copy.38, bf16[256,1792]{0,1:T(8,128)(2,1)S(1)} %copy.35), kind=kLoop, calls=%fused_computation.13 | loop fusion | flops 9175040 | bytes 8257536 | tf_op jit(solution)/shard_map/convert_element_type | solution.py:28
  472.8 2.7 copy.40
  475.6 0.0 copy-start.1
  475.6 2.3 copy.41
  477.9 0.0 copy-done.1
  477.9 1.4 copy.42
  479.2 70.4 %reduce-scatter.3.cloned.1.call-done = bf16[256,256]{1,0:T(8,128)(2,1)} async-done(((bf16[256,4096]{1,0:T(8,128)(2,1)}), bf16[256,256]{1,0:T(8,128)(2,1)}) %reduce-scatter.3.cloned.1.call-update) | async-done | bytes 131088 | tf_op jit(solution)/shard_map/reduce_scatter | solution.py:60
Async XLA Ops:
  7.2 252.7 %copy-start = (bf16[256,4096]{1,0:T(8,128)(2,1)S(1)}, bf16[256,4096]{1,0:T(8,128)(2,1)}, u32[]{:S(2)}) copy-start(bf16[256,4096]{1,0:T(8,128)(2,1)} %param.7) | copy-start | bytes 6291460
  7.2 162.5 %all-gather.3.cloned.1.call-start = ((), (), s32[]{:S(2)}) async-start(), calls=%async_computation.2 | async-start | bytes 15597568 | tf_op jit(solution)/shard_map/all_gather | solution.py:41
  7.9 458.9 %reduce-scatter.5.cloned.1.call-start = ((), (), s32[]{:S(2)}) async-start(), calls=%async_computation.4 | async-start | bytes 15597568 | tf_op jit(solution)/shard_map/reduce_scatter | solution.py:67
  267.8 0.8 copy-start.2
  276.8 1.0 copy-start.3
  276.9 272.7 %reduce-scatter.3.cloned.1.call-start = ((), (), s32[]{:S(2)}) async-start(), calls=%async_computation.3 | async-start | bytes 2228224 | tf_op jit(solution)/shard_map/reduce_scatter | solution.py:60
  475.6 2.3 copy-start.1
Sparse Core Ops, SparseCore 0:
  10.7 158.9 all-gather.2
  277.0 189.7 reduce-scatter.4
  470.1 79.4 reduce-scatter.2
where the time goes:
time: 562 us; the launch traced here: 556 us
  waiting for transfers between devices  377 us (67%)
  local copies, waits for them, and re-layouts  60 us (11%)
  other arithmetic  54.5 us (10%)
  matrix products  25.9 us (5%)
  blocking collectives  24.7 us (4%)
  between operations  13.8 us (2%)
    reduce_scatter x1, waiting for transfers between devices, body(): lax.psum_scatter((product * grad_scale).astype(jnp.bfloat16), ('opt', 'dp...  171 us
    all_gather x1, waiting for transfers between devices, body(): lax.all_gather(weight_codes, ('opt', 'dp'), axis=0, tiled=True)  135 us
    reduce_scatter x1, waiting for transfers between devices, body(): lax.psum_scatter(partial_tokens.astype(jnp.bfloat16), 'tensor', scatter_d...  70.4 us
    convert_element_type x1, other arithmetic, dequantize(): return scaled.reshape(blocks * inner_rows, columns).astype(jnp.bfloat16)  30.6 us
    reshape x1, local copies, waits for them, and re-layouts, dequantize(): weight_codes.astype(jnp.float32)  29.5 us
    all_gather x1, blocking collectives, body(): lax.all_gather(scales.astype(jnp.bfloat16), ('opt', 'dp'), axis=0, tiled=...  24.7 us
    unnamed x16, local copies, waits for them, and re-layouts  16.9 us
    reshape x1, other arithmetic, dequantize(): weight_codes.astype(jnp.float32)  16.5 us
  transfers between devices with their start and end apart: 3, of which 3 were waited for; matrix products, arithmetic and copies ran while one was open for 6% of the time, Pallas kernels for 0%

commit v1 on v0

v1 whole, which is shorter than its diff:
```python
import jax
import jax.numpy as jnp
from jax import lax
from jax.experimental import pallas as pl
from jax.experimental.pallas import tpu as pltpu
from jax.sharding import PartitionSpec as P

F32 = jnp.float32
BF16 = jnp.bfloat16
OT = ("opt", "tensor")
VMEM = pl.BlockSpec(memory_space=pltpu.VMEM)
SMEM = pl.BlockSpec(memory_space=pltpu.SMEM)
LIMIT = 48 * 1024 * 1024

X_GROUPS = [[0, 2, 4, 6], [1, 3, 5, 7]]
EIGHTHS = [list(range(8)), list(range(8, 16))]


def along_x(a, step):
    return lax.ppermute(a, "dp", [(x * 2 + c, (x + step) % 4 * 2 + c) for x in range(4) for c in range(2)])


def other_core(a):
    return lax.ppermute(a, "dp", [(i, i ^ 1) for i in range(8)])


def other_opt(a):
    return lax.ppermute(a, "opt", [(0, 1), (1, 0)])


def along_y(a, step):
    return lax.ppermute(a, "tensor", [(z * 4 + y, z * 4 + (y + step) % 4) for z in range(4) for y in range(4)])


def along_z(a, step):
    return lax.ppermute(a, OT, [(z * 4 + y, (z + step) % 8 * 4 + y) for z in range(8) for y in range(4)])


def params():
    return pltpu.CompilerParams(vmem_limit_bytes=LIMIT)


def low_lanes(shape):
    return lax.broadcasted_iota(jnp.int32, shape, 1) < 64


def prepare_kernel(opt_ref, scale_ref, code_ref, own_ref, send_ref):
    first = opt_ref[0] == 0
    low = low_lanes((128, 128))

    def put(rows, at, half0, half1):
        own_ref[rows, at : at + 128] = jnp.where(first, half0, half1).astype(BF16)
        send_ref[rows, at : at + 128] = jnp.where(first, half1, half0).astype(BF16)

    for b in range(2):
        rows = slice(b * 128, b * 128 + 128)

        def tile(j):
            return code_ref[b, :, j * 128 : j * 128 + 128].astype(F32) * scale_ref[b, j]

        for part in range(2):
            for j in range(3):
                put(rows, part * 384 + j * 128, tile(part * 7 + j), tile(part * 7 + 4 + j))
        gate, up = tile(3), tile(10)
        put(
            rows,
            768,
            jnp.where(low, gate, pltpu.roll(up, 64, 1)),
            jnp.where(low, pltpu.roll(gate, 64, 1), up),
        )


def prepare(opt, scales, codes):
    out = jax.ShapeDtypeStruct((256, 896), BF16)
    return pl.pallas_call(
        prepare_kernel,
        out_shape=(out, out),
        in_specs=[SMEM, SMEM, VMEM],
        out_specs=(VMEM, VMEM),
        compiler_params=params(),
        cost_estimate=pl.CostEstimate(flops=1 << 19, bytes_accessed=1 << 21, transcendentals=0),
    )(opt, scales, codes)


def split_kernel(core_ref, keep_in, send_in, keep_ref, send_ref):
    keep_ref[...] = keep_in[...]
    send_ref[...] = send_in[...]


def split_tokens(core, tokens):
    out = jax.ShapeDtypeStruct((256, 2048), BF16)
    return pl.pallas_call(
        split_kernel,
        out_shape=(out, out),
        grid_spec=pltpu.PrefetchScalarGridSpec(
            num_scalar_prefetch=1,
            grid=(8,),
            in_specs=[
                pl.BlockSpec((256, 256), lambda i, core: (0, 2 * i + core[0])),
                pl.BlockSpec((256, 256), lambda i, core: (0, 2 * i + 1 - core[0])),
            ],
            out_specs=(
                pl.BlockSpec((256, 256), lambda i, core: (0, i)),
                pl.BlockSpec((256, 256), lambda i, core: (0, i)),
            ),
        ),
        compiler_params=params(),
        cost_estimate=pl.CostEstimate(flops=0, bytes_accessed=1 << 22, transcendentals=0),
    )(core, tokens, tokens)


def project_kernel(at_ref, tok_ref, *refs):
    pieces, own_ref, send_ref = refs[:-2], refs[-2], refs[-1]
    for half in range(2):
        rows = slice(half * 256, half * 256 + 256)
        total = None
        for i, piece in enumerate(pieces):
            depth = piece.shape[0]
            columns = pl.ds(pl.multiple_of(at_ref[i] * 128, 128), depth)
            term = jnp.dot(tok_ref[rows, columns], piece[...], preferred_element_type=F32)
            total = term if total is None else total + term
        if half == 0:
            own_ref[...] = total
        else:
            send_ref[...] = total.astype(BF16)


def project(at, tok, pieces):
    return pl.pallas_call(
        project_kernel,
        out_shape=(jax.ShapeDtypeStruct((256, 896), F32), jax.ShapeDtypeStruct((256, 896), BF16)),
        in_specs=[SMEM] + [VMEM] * (1 + len(pieces)),
        out_specs=(VMEM, VMEM),
        compiler_params=params(),
        cost_estimate=pl.CostEstimate(flops=2 * 512 * 2048 * 896, bytes_accessed=7 << 20, transcendentals=0),
    )(at, tok, *pieces)


def swiglu_kernel(own_ref, recv_ref, up_grad_ref, hidden_ref, grad_ref):
    def parts(gate, up, upstream):
        s = 1.0 / (1.0 + jnp.exp(-gate))
        act = gate * s
        return act * up, upstream * up * s * (1.0 + gate * (1.0 - s)), upstream * act

    def projected(at):
        return own_ref[:, at : at + 128] + recv_ref[:, at : at + 128].astype(F32)

    for j in range(3):
        at = j * 128
        hidden, grad_gate, grad_up = parts(
            projected(at), projected(384 + at), up_grad_ref[:, at : at + 128].astype(F32)
        )
        hidden_ref[:, at : at + 128] = hidden.astype(BF16)
        grad_ref[:, at : at + 128] = grad_gate.astype(BF16)
        grad_ref[:, 384 + at : 384 + at + 128] = grad_up.astype(BF16)
    mixed = projected(768)
    hidden, grad_gate, grad_up = parts(mixed, pltpu.roll(mixed, 64, 1), up_grad_ref[:, 384:512].astype(F32))
    hidden_ref[:, 384:512] = hidden.astype(BF16)
    grad_ref[:, 768:896] = jnp.where(low_lanes(mixed.shape), grad_gate, pltpu.roll(grad_up, 64, 1)).astype(BF16)


def swiglu(own, recv, up_grad):
    return pl.pallas_call(
        swiglu_kernel,
        out_shape=(jax.ShapeDtypeStruct((256, 512), BF16), jax.ShapeDtypeStruct((256, 896), BF16)),
        in_specs=[VMEM] * 3,
        out_specs=(VMEM, VMEM),
        compiler_params=params(),
        cost_estimate=pl.CostEstimate(flops=256 * 448 * 16, bytes_accessed=5 << 19, transcendentals=256 * 448),
    )(own, recv, up_grad)


def token_grad_kernel(which_ref, block_ref, g0_ref, g1_ref, *refs):
    weights, extra, out_ref = refs[:4], refs[4:-1], refs[-1]
    i = pl.program_id(0)
    for a in range(4):

        @pl.when(which_ref[i] == a)
        def _():
            for half, g_ref in enumerate((g0_ref, g1_ref)):
                rows = slice(half * 256, half * 256 + 256)
                term = lax.dot_general(
                    g_ref[...], weights[a][0], (((1,), (1,)), ((), ())), preferred_element_type=F32
                )
                if extra:
                    term = term + extra[0][0, rows].astype(F32) * jnp.where(i < 2, 1.0, 0.0)
                out_ref[0, rows] = term.astype(BF16)


def token_grad(which, block, g0, g1, weights, extra=None):
    steps = which.shape[0]

    def of(a):
        return lambda i, which, block: (jnp.where(which[i] == a, block[i], 0), 0, 0)

    in_specs = [pl.BlockSpec((256, 896), lambda i, which, block: (0, 0))] * 2
    in_specs += [pl.BlockSpec((1, 256, 896), of(a)) for a in range(4)]
    args = [g0, g1] + [w.reshape(4, 256, 896) for w in weights]
    if extra is not None:
        in_specs.append(pl.BlockSpec((1, 512, 256), lambda i, which, block: (jnp.minimum(i, 1), 0, 0)))
        args.append(extra)
    return pl.pallas_call(
        token_grad_kernel,
        out_shape=jax.ShapeDtypeStruct((steps, 512, 256), BF16),
        grid_spec=pltpu.PrefetchScalarGridSpec(
            num_scalar_prefetch=2,
            grid=(steps,),
            in_specs=in_specs,
            out_specs=pl.BlockSpec((1, 512, 256), lambda i, which, block: (i, 0, 0)),
        ),
        compiler_params=params(),
        cost_estimate=pl.CostEstimate(
            flops=2 * 512 * 896 * 256 * steps, bytes_accessed=steps * 800000 + 1000000, transcendentals=0
        ),
    )(which, block, *args)


def weight_grad_kernel(half_ref, t0_ref, t1_ref, g0, g1, g2, g3, out_ref):
    total = None
    for rows, t_ref, g in ((0, t0_ref, g0), (256, t0_ref, g1), (0, t1_ref, g2), (256, t1_ref, g3)):
        term = lax.dot_general(
            t_ref[rows : rows + 256, :], g[...], (((0,), (0,)), ((), ())), preferred_element_type=F32
        )
        total = term if total is None else total + term
    out_ref[...] = (total * (1.0 / 64.0)).astype(BF16)


def weight_grad(half, t0, t1, grads):
    tok = pl.BlockSpec((512, 256), lambda i, half: (0, half[0] * 4 + i))
    whole = pl.BlockSpec((256, 896), lambda i, half: (0, 0))
    return pl.pallas_call(
        weight_grad_kernel,
        out_shape=jax.ShapeDtypeStruct((1024, 896), BF16),
        grid_spec=pltpu.PrefetchScalarGridSpec(
            num_scalar_prefetch=1,
            grid=(4,),
            in_specs=[tok, tok] + [whole] * 4,
            out_specs=pl.BlockSpec((256, 896), lambda i, half: (i, 0)),
        ),
        compiler_params=params(),
        cost_estimate=pl.CostEstimate(flops=2 * 1024 * 1024 * 896, bytes_accessed=6 << 20, transcendentals=0),
    )(half, t0, t1, *grads)


def adam_kernel(opt_ref, mine_ref, recv_ref, master_ref, m_ref, v_ref, master_out, m_out, v_out):
    first = opt_ref[0] == 0
    low = low_lanes((mine_ref.shape[0], 128))
    fix_one = 1.0 - 0.9**20.0
    fix_two = 1.0 - 0.95**20.0

    def tile(half, at):
        mine, recv = (r[:, at : at + 128].astype(F32) for r in (mine_ref, recv_ref))
        return jnp.where(first, mine, recv) if half == 0 else jnp.where(first, recv, mine)

    mixed0, mixed1 = tile(0, 768), tile(1, 768)
    for j in range(14):
        part, k = divmod(j, 7)
        if k < 3:
            grads = tile(0, part * 384 + k * 128)
        elif k > 3:
            grads = tile(1, part * 384 + (k - 4) * 128)
        elif part == 0:
            grads = jnp.where(low, mixed0, pltpu.roll(mixed1, 64, 1))
        else:
            grads = jnp.where(low, pltpu.roll(mixed0, 64, 1), mixed1)
        at = slice(j * 128, j * 128 + 128)
        master = master_ref[:, at]
        one = 0.9 * m_ref[:, at].astype(F32) + 0.1 * grads
        two = 0.95 * v_ref[:, at].astype(F32) + 0.05 * grads * grads
        direction = one / fix_one / (jnp.sqrt(two / fix_two) + 1e-08)
        master_out[:, at] = master - 0.001 * (direction + 0.1 * master)
        m_out[:, at] = one.astype(BF16)
        v_out[:, at] = two.astype(BF16)


def adam(opt, mine, recv, master, first_moment, second_moment):
    half = pl.BlockSpec((32, 896), lambda i, opt: (i, 0))
    whole = pl.BlockSpec((32, 1792), lambda i, opt: (i, 0))
    return pl.pallas_call(
        adam_kernel,
        out_shape=(
            jax.ShapeDtypeStruct((256, 1792), F32),
            jax.ShapeDtypeStruct((256, 1792), BF16),
            jax.ShapeDtypeStruct((256, 1792), BF16),
        ),
        grid_spec=pltpu.PrefetchScalarGridSpec(
            num_scalar_prefetch=1,
            grid=(8,),
            in_specs=[half, half, whole, whole, whole],
            out_specs=(whole, whole, whole),
        ),
        compiler_params=params(),
        cost_estimate=pl.CostEstimate(flops=256 * 1792 * 16, bytes_accessed=9 << 20, transcendentals=256 * 1792),
    )(opt, mine, recv, master, first_moment, second_moment)


def ring_gather(block):
    before, after = along_x(block, 1), along_x(block, -1)
    far0, far1 = along_x(before[:128], 1), along_x(after[128:], -1)
    return [block, before, after, far0, far1]


def body(tokens, grad_hidden, weight_codes, scales, master, first_moment, second_moment):
    o = lax.axis_index("opt")
    dp = lax.axis_index("dp")
    t = lax.axis_index("tensor")
    x, c = dp // 2, dp % 2
    zl, y = t // 4, t % 4
    z = o * 4 + zl
    opt = o.astype(jnp.int32).reshape(1)
    core = c.astype(jnp.int32).reshape(1)

    w_own, w_send = prepare(opt, scales, weight_codes)
    w_recv = other_opt(w_send)
    near = ring_gather(w_own)
    far = ring_gather(w_recv)

    keep, send = split_tokens(core, tokens)
    t_own = jnp.concatenate([keep, other_core(send)], axis=0)
    eighth = lax.dynamic_slice_in_dim(t_own, (t % 8) * 64, 64, axis=0)
    t_far = lax.all_gather(other_opt(eighth), "tensor", axis_index_groups=EIGHTHS, axis=0, tiled=True)

    lower = grad_hidden[:, :512]
    upper = jnp.concatenate([grad_hidden[:, 512:], grad_hidden[:, 448:512], grad_hidden[:, 384:448]], axis=1)
    up_own = jnp.where(o == 0, lower, upper)
    up_far = other_opt(jnp.where(o == 0, upper, lower))

    xs = [x, (x + 3) % 4, (x + 1) % 4, (x + 2) % 4]
    rows = [2 * v for v in xs] + [2 * xs[3] + 1]
    at = jnp.stack([o * 8 + v for v in rows] + [(1 - o) * 8 + v for v in rows]).astype(jnp.int32)

    own0, send0 = project(at, t_own, near + far)
    recv0 = other_core(send0)
    own1, send1 = project(at, t_far, near + far)
    recv1 = other_core(send1)
    hidden0, g0 = swiglu(own0, recv0, up_own)
    hidden1, g2 = swiglu(own1, recv1, up_far)
    hidden_recv = other_opt(hidden1)
    half0 = jnp.where(o == 0, hidden0, hidden_recv)
    half1 = jnp.where(o == 0, hidden_recv, hidden0)
    hidden = jnp.concatenate([half0[:, :448], half1[:, 384:448], half1[:, :384]], axis=1)
    g1, g3 = other_core(g0), other_core(g2)

    w_near, w_far = jnp.concatenate(near, axis=0), jnp.concatenate(far, axis=0)
    weights = [w_near, w_far, other_core(w_near), other_core(w_far)]

    def table(k):
        target = (y + k) % 4
        core_is = (target % 2 != c).astype(jnp.int32) * 2
        which, block = [], []
        for zt in range(4):
            xt = (zt % 2) * 2 + target // 2
            which.append(core_is + (zt // 2 != o).astype(jnp.int32))
            d = (xt - x) % 4
            block.append(jnp.where(d == 0, 0, jnp.where(d == 3, 1, jnp.where(d == 1, 2, 3))))
        return jnp.stack(which).astype(jnp.int32), jnp.stack(block).astype(jnp.int32)

    w2, b2 = table(2)
    w1, b1 = table(1)
    w3, b3 = table(3)
    w0, b0 = table(0)
    forth = along_y(token_grad(w2[:2], b2[:2], g0, g2, weights), 1)
    back = along_y(token_grad(w2[2:], b2[2:], g0, g2, weights), -1)
    swap = jnp.array([2, 3, 0, 1])
    right = along_y(token_grad(w1, b1, g0, g2, weights, forth), 1)
    left = along_y(token_grad(w3[swap], b3[swap], g0, g2, weights, back), -1)
    mine = token_grad(w0, b0, g0, g2, weights)

    def piece(k):
        zt = (z + k) % 8
        zlt, hi = zt % 4, (zt // 4 != o).astype(jnp.int32)

        def of(a, first):
            return lax.dynamic_slice(a, (first, hi * 256, 0), (1, 256, 256))[0].astype(F32)

        return of(mine, zlt) + of(right, zlt) + of(left, (zlt + 2) % 4)

    up = along_z(piece(4).astype(BF16), 1)
    down = along_z(piece(5).astype(BF16), -1)
    up = along_z((up.astype(F32) + piece(3)).astype(BF16), 1)
    down = along_z((down.astype(F32) + piece(6)).astype(BF16), -1)
    up = along_z((up.astype(F32) + piece(2)).astype(BF16), 1)
    down = along_z((down.astype(F32) + piece(7)).astype(BF16), -1)
    up = along_z((up.astype(F32) + piece(1)).astype(BF16), 1)
    grad_tokens = (piece(0) + up.astype(F32) + down.astype(F32)).astype(BF16)

    all_g = (g0, g1, g2, g3)
    dw_far = lax.psum_scatter(
        weight_grad(1 - opt, t_own, t_far, all_g), "dp", scatter_dimension=0, axis_index_groups=X_GROUPS, tiled=True
    )
    dw_own = lax.psum_scatter(
        weight_grad(opt, t_own, t_far, all_g), "dp", scatter_dimension=0, axis_index_groups=X_GROUPS, tiled=True
    )
    new_master, new_first, new_second = adam(opt, dw_own, other_opt(dw_far), master, first_moment, second_moment)
    return hidden, grad_tokens, new_master, new_first, new_second


def solution(mesh):
    rows = ("opt", "dp")
    in_specs = (
        P(rows, None),
        P(rows, "tensor"),
        P(rows, None, "tensor"),
        P(rows, "tensor"),
        P(rows, "tensor"),
        P(rows, "tensor"),
        P(rows, "tensor"),
    )
    out_specs = (P(rows, "tensor"),) * 5
    return jax.shard_map(body, mesh=mesh, in_specs=in_specs, out_specs=out_specs, check_vma=False)
```

time: 562 us -> 293 us (0.52)
  waiting for transfers between devices: 377 us -> 93.6 us
  starting transfers between devices: 0.3 us -> 88.3 us
  Pallas kernels: 0 us -> 50.9 us
  other arithmetic: 54.5 us -> 12.3 us
  local copies, waits for them, and re-layouts: 60 us -> 28.5 us
  matrix products: 25.9 us -> 0 us
  blocking collectives: 24.7 us -> 0 us
    reduce_scatter x2, waiting for transfers between devices: 241 us -> 0.01 us  [the longest x1 0.01 us: body(): lax.psum_scatter(weight_grad(1 - opt, t_own, t_far, all_g), 'dp', scatter...]
    all_gather x1, waiting for transfers between devices: 135 us -> 3.28 us  [body(): lax.all_gather(other_opt(eighth), 'tensor', axis_index_groups=EIGHTHS, ax...]
    ppermute x0 -> x31, waiting for transfers between devices: none -> 90.2 us  [the longest x5 44.6 us: other_opt(): return lax.ppermute(a, 'opt', [(0, 1), (1, 0)])]
    ppermute x0 -> x31, starting transfers between devices: none -> 88.2 us  [the longest x5 39.8 us: other_opt(): return lax.ppermute(a, 'opt', [(0, 1), (1, 0)])]
    pallas_call x0 -> x14, Pallas kernels: none -> 50.9 us  [the longest x5 21.7 us: token_grad(): pl.pallas_call(token_grad_kernel, out_shape=jax.ShapeDtypeStruct((steps,...]
    reshape x1 -> x0, local copies, waits for them, and re-layouts: 29.5 us -> none  [dequantize(): weight_codes.astype(jnp.float32)]
    convert_element_type x2 -> x5, other arithmetic: 36.6 us -> 7.57 us  [the longest x1 2.05 us: body(): up = along_z((up.astype(F32) + piece(1)).astype(BF16), 1)]
    dot_general x3 -> x0, matrix products: 25.9 us -> none  [the longest x1 10.4 us: body(): lax.dot_general(grad_proj, weights, (((1,), (1,)), ((), ())), preferred_e...]
  transfers between devices with their start and end apart: 3 -> 34, of which waited for: 3 -> 18; matrix products, arithmetic and copies ran while one was open for 6% -> 11% of each run, Pallas kernels for 0% -> 13%
where the time goes in v1:
time: 293 us; the launch traced here: 288 us
  waiting for transfers between devices  93.6 us (32%)
  starting transfers between devices  88.3 us (30%)
  Pallas kernels  50.9 us (17%)
  local copies, waits for them, and re-layouts  28.5 us (10%)
  between operations  14.3 us (5%)
  other arithmetic  12.3 us (4%)
    ppermute x5, waiting for transfers between devices, other_opt(): return lax.ppermute(a, 'opt', [(0, 1), (1, 0)])  44.6 us
    ppermute x5, starting transfers between devices, other_opt(): return lax.ppermute(a, 'opt', [(0, 1), (1, 0)])  39.8 us
    ppermute x7, starting transfers between devices, along_z(): lax.ppermute(a, OT, [(z * 4 + y, (z + step) % 8 * 4 + y) for z in range(8...  25.3 us
    ppermute x4, waiting for transfers between devices, along_y(): lax.ppermute(a, 'tensor', [(z * 4 + y, z * 4 + (y + step) % 4) for z in r...  23 us
    pallas_call x5, Pallas kernels, token_grad(): pl.pallas_call(token_grad_kernel, out_shape=jax.ShapeDtypeStruct((steps,...  21.7 us
    unnamed x65, local copies, waits for them, and re-layouts  15.9 us
    ppermute x4, starting transfers between devices, along_y(): lax.ppermute(a, 'tensor', [(z * 4 + y, z * 4 + (y + step) % 4) for z in r...  13.5 us
    pallas_call x2, Pallas kernels, project(): pl.pallas_call(project_kernel, out_shape=(jax.ShapeDtypeStruct((256, 896)...  10 us
  transfers between devices with their start and end apart: 34, of which 18 were waited for; matrix products, arithmetic and copies ran while one was open for 11% of the time, Pallas kernels for 13%

profile of v1, /device:TPU:14, one launch (start us, length us, event | category | flops | bytes accessed | tf_op | source)
XLA Modules:
  0.0 288.0 jit_solution(11492869657577845419)
XLA Ops:
  7.2 1.6 copy-done.3
  8.8 3.0 %shard_map.119 = (bf16[256,2048]{1,0:T(8,128)(2,1)S(1)}, bf16[256,2048]{1,0:T(8,128)(2,1)}) custom-call(s32[1]{0:T(128)} %bitcast.10.core_ref, bf16[256,4096]{1,0:T(8,128)(2,1)S(1)} %copy-done.3, bf16[256,4096]{1,0:T(8,128)(2,1)S(1)} %copy-done.3), custom_call_target="tpu_custom_call" | custom-call | bytes 4194304 | tf_op jit(solution)/shard_map/pallas_call | solution.py:92
  12.0 2.9 collective-permute-done
  14.9 1.3 constant_dynamic-update-slice_fusion.tok_ref.t0_ref
  16.2 7.3 %collective-permute-start.11 = (bf16[64,2048]{1,0:T(8,128)(2,1)S(1)}, bf16[64,2048]{1,0:T(8,128)(2,1)S(1)}, u32[]{:S(2)}, u32[]{:S(2)}) collective-permute-start(bf16[64,2048]{1,0:T(8,128)(2,1)S(1)} %constant_dynamic-slice_fusion), channel_id=1, source_target_pairs={{0,128},{128,0},{1,129},{129,1},{2,130},{130,2},{3,131},{131,3},{4... | collective-permute-start | bytes 786440 | tf_op jit(solution)/shard_map/ppermute | solution.py:28
  23.5 7.7 %collective-permute-done.11 = bf16[64,2048]{1,0:T(8,128)(2,1)S(1)} collective-permute-done((bf16[64,2048]{1,0:T(8,128)(2,1)S(1)}, bf16[64,2048]{1,0:T(8,128)(2,1)S(1)}, u32[]{:S(2)}, u32[]{:S(2)}) %collective-permute-start.11) | collective-permute-done | bytes 262176 | tf_op jit(solution)/shard_map/ppermute | solution.py:28
  32.0 1.6 shard_map.120
  33.6 9.5 %collective-permute-start.5 = (bf16[256,896]{1,0:T(8,128)(2,1)S(1)}, bf16[256,896]{1,0:T(8,128)(2,1)}, u32[]{:S(2)}, u32[]{:S(2)}) collective-permute-start(bf16[256,896]{1,0:T(8,128)(2,1)S(1)} %get-tuple-element.23), channel_id=1, source_target_pairs={{0,128},{128,0},{1,129},{129,1},{2,130},{130,2},{3,131},{131,3},{4... | collective-permute-start | bytes 1376264 | tf_op jit(solution)/shard_map/ppermute | solution.py:28
  43.6 1.5 collective-permute-start.2
  45.1 13.7 %collective-permute-done.5.refs_5_ = bf16[256,896]{1,0:T(8,128)(2,1)} collective-permute-done((bf16[256,896]{1,0:T(8,128)(2,1)S(1)}, bf16[256,896]{1,0:T(8,128)(2,1)}, u32[]{:S(2)}, u32[]{:S(2)}) %collective-permute-start.5) | collective-permute-done | bytes 458784 | tf_op jit(solution)/shard_map/ppermute | solution.py:28
  59.4 1.5 collective-permute-start.7
  60.9 1.6 slice.56
  62.5 1.7 collective-permute-start.3
  64.2 1.7 slice.57
  66.2 1.6 collective-permute-done.6.refs_6_
  68.7 2.5 collective-permute-start.8
  72.0 1.6 fusion.9
  73.6 1.4 collective-permute-done.8.refs_8_
  75.0 4.5 %collective-permute-done.9.refs_9_ = bf16[128,896]{1,0:T(8,128)(2,1)} collective-permute-done((bf16[128,896]{1,0:T(8,128)(2,1)}, bf16[128,896]{1,0:T(8,128)(2,1)}, u32[]{:S(2)}, u32[]{:S(2)}) %collective-permute-start.9) | collective-permute-done | bytes 229408 | tf_op jit(solution)/shard_map/ppermute | solution.py:20
  79.5 5.0 %shard_map.121 = (f32[256,896]{1,0:T(8,128)S(1)}, bf16[256,896]{1,0:T(8,128)(2,1)S(1)}) custom-call(s32[10]{0:T(128)S(1)} %stack.133.at_ref, bf16[512,2048]{1,0:T(8,128)(2,1)} %copy-done, bf16[256,896]{1,0:T(8,128)(2,1)} %get-tuple-element.22.refs_0_, bf16[256,896]{1,0:T(8,128)(2,1)} %collective-permute-done.1.refs_1_, ...), custom_call_target="tpu_custom_call" | custom-call | flops 1879048192 | bytes 7340032 | tf_op jit(solution)/shard_map/pallas_call | solution.py:129
  85.7 3.3 %all-gather.2.cloned.1.call-done.tok_ref.t1_ref = bf16[512,2048]{1,0:T(8,128)(2,1)} async-done(((bf16[64,2048]{1,0:T(8,128)(2,1)}), bf16[512,2048]{1,0:T(8,128)(2,1)}) %all-gather.2.cloned.1.call-update) | async-done | bytes 2097168 | tf_op jit(solution)/shard_map/all_gather | solution.py:321
  89.0 5.0 %shard_map.123 = (f32[256,896]{1,0:T(8,128)S(1)}, bf16[256,896]{1,0:T(8,128)(2,1)S(1)}) custom-call(s32[10]{0:T(128)S(1)} %stack.133.at_ref, bf16[512,2048]{1,0:T(8,128)(2,1)} %all-gather.2.cloned.1.call-done.tok_ref.t1_ref, bf16[256,896]{1,0:T(8,128)(2,1)} %get-tuple-element.22.refs_0_, bf16[256,896]{1,0:T(8,128)(2,1)} %collective-permute-done.1.refs_1_, ...), custom_call_target="tpu_custom_call" | custom-call | flops 1879048192 | bytes 7340032 | tf_op jit(solution)/shard_map/pallas_call | solution.py:129
  94.1 1.1 broadcast_select_fusion.2
  95.2 2.6 collective-permute-start.13
  98.5 9.6 %collective-permute-done.13.up_grad_ref = bf16[256,512]{1,0:T(8,128)(2,1)S(1)} collective-permute-done((bf16[256,512]{1,0:T(8,128)(2,1)S(1)}, bf16[256,512]{1,0:T(8,128)(2,1)S(1)}, u32[]{:S(2)}, u32[]{:S(2)}) %collective-permute-start.13) | collective-permute-done | bytes 262176 | tf_op jit(solution)/shard_map/ppermute | solution.py:28
  109.2 1.8 collective-permute-done.29.g3
  111.1 5.2 %shard_map.131 = bf16[1024,896]{1,0:T(8,128)(2,1)} custom-call(s32[1]{0:T(128)S(6)} %sub.120.half_ref, bf16[512,2048]{1,0:T(8,128)(2,1)S(1)} %copy-done.1, bf16[512,2048]{1,0:T(8,128)(2,1)} %all-gather.2.cloned.1.call-done.tok_ref.t1_ref, bf16[256,896]{1,0:T(8,128)(2,1)S(1)} %get-tuple-element.30.g0_ref.g0, bf16[256,896]{1,0:T(8,128)(2,1)S(1)} %collective-permute-done.28.g1, ...), custom_call_target="tpu_custom_call" | custom-call | flops 1879048192 | bytes 6291456 | tf_op jit(solution)/shard_map/pallas_call | solution.py:231
  117.1 1.9 constant_dynamic-update-slice_fusion.6
  119.0 1.1 constant_dynamic-update-slice_fusion.11
  120.1 1.9 constant_dynamic-update-slice_fusion.5
  122.0 1.9 constant_dynamic-update-slice_fusion.4
  124.6 1.6 constant_dynamic-update-slice_fusion.2
  128.1 2.2 collective-permute-done.15
  130.3 2.4 collective-permute-done.16
  132.8 3.8 %shard_map.128 = bf16[2,512,256]{2,1,0:T(8,128)(2,1)} custom-call(s32[2]{0:T(128)S(1)} %pad_add_fusion.8.which_ref, s32[2]{0:T(128)S(1)} %get-tuple-element.50.block_ref, bf16[256,896]{1,0:T(8,128)(2,1)S(1)} %get-tuple-element.30.g0_ref.g0, bf16[256,896]{1,0:T(8,128)(2,1)S(1)} %get-tuple-element.31.g1_ref.g2, bf16[4,256,896]{2,1,0:T(8,128)(2,1)} %bitcast.16.refs_0_, ...), custom_call_target="tpu_custom_call" | custom-call | flops 469762048 | bytes 2600000 | tf_op jit(solution)/shard_map/pallas_call | solution.py:202
  136.6 4.3 %shard_map.130 = bf16[1024,896]{1,0:T(8,128)(2,1)S(1)} custom-call(s32[1]{0:T(128)} %bitcast.11.opt_ref.half_ref, bf16[512,2048]{1,0:T(8,128)(2,1)S(1)} %copy-done.2, bf16[512,2048]{1,0:T(8,128)(2,1)} %all-gather.2.cloned.1.call-done.tok_ref.t1_ref, bf16[256,896]{1,0:T(8,128)(2,1)S(1)} %get-tuple-element.30.g0_ref.g0, ...), custom_call_target="tpu_custom_call" | custom-call | flops 1879048192 | bytes 6291456 | tf_op jit(solution)/shard_map/pallas_call | solution.py:231
  140.9 1.2 copy-done.4
  142.2 3.0 %shard_map.126 = bf16[2,512,256]{2,1,0:T(8,128)(2,1)S(1)} custom-call(s32[2]{0:T(128)S(1)} %get-tuple-element.49.which_ref, s32[2]{0:T(128)S(1)} %get-tuple-element.50.block_ref, bf16[256,896]{1,0:T(8,128)(2,1)S(1)} %get-tuple-element.30.g0_ref.g0, bf16[256,896]{1,0:T(8,128)(2,1)S(1)} %get-tuple-element.31.g1_ref.g2, bf16[4,256,896]{2,1,0:T(8,128)(2,1)} %bitcast.16.refs_0_, ...), custom_call_target="tpu_custom_call" | custom-call | flops 469762048 | bytes 2600000 | tf_op jit(solution)/shard_map/pallas_call | solution.py:202
  145.2 11.3 %collective-permute-start.17 = (bf16[2,512,256]{2,1,0:T(8,128)(2,1)S(1)}, bf16[2,512,256]{2,1,0:T(8,128)(2,1)}, u32[]{:S(2)}, u32[]{:S(2)}) collective-permute-start(bf16[2,512,256]{2,1,0:T(8,128)(2,1)S(1)} %shard_map.126), channel_id=1, source_target_pairs={{0,1},{1,2},{2,3},{3,0},{4,5},{5,6},{6,7},{7,4},{8,9},{9,10},{10,1... | collective-permute-start | bytes 1572872 | tf_op jit(solution)/shard_map/ppermute | solution.py:32
  158.6 5.4 %shard_map.129 = bf16[4,512,256]{2,1,0:T(8,128)(2,1)} custom-call(s32[4]{0:T(128)S(1)} %gather_fusion, s32[4]{0:T(128)S(1)} %gather_fusion.1, bf16[256,896]{1,0:T(8,128)(2,1)S(1)} %get-tuple-element.30.g0_ref.g0, bf16[256,896]{1,0:T(8,128)(2,1)S(1)} %get-tuple-element.31.g1_ref.g2, bf16[4,256,896]{2,1,0:T(8,128)(2,1)} %bitcast.16.refs_0_, ...), custom_call_target="tpu_custom_call" | custom-call | flops 939524096 | bytes 4200000 | tf_op jit(solution)/shard_map/pallas_call | solution.py:202
  164.1 4.6 %collective-permute-done.17.refs_4_ = bf16[2,512,256]{2,1,0:T(8,128)(2,1)} collective-permute-done((bf16[2,512,256]{2,1,0:T(8,128)(2,1)S(1)}, bf16[2,512,256]{2,1,0:T(8,128)(2,1)}, u32[]{:S(2)}, u32[]{:S(2)}) %collective-permute-start.17) | collective-permute-done | bytes 524320 | tf_op jit(solution)/shard_map/ppermute | solution.py:32
  168.6 4.9 %shard_map.127 = bf16[4,512,256]{2,1,0:T(8,128)(2,1)} custom-call(s32[4]{0:T(128)S(1)} %get-tuple-element.47.which_ref, s32[4]{0:T(128)S(1)} %get-tuple-element.48.block_ref, bf16[256,896]{1,0:T(8,128)(2,1)S(1)} %get-tuple-element.30.g0_ref.g0, bf16[256,896]{1,0:T(8,128)(2,1)S(1)} %get-tuple-element.31.g1_ref.g2, bf16[4,256,896]{2,1,0:T(8,128)(2,1)} %bitcast.16.refs_0_, ...), custom_call_target="tpu_custom_call" | custom-call | flops 939524096 | bytes 4200000 | tf_op jit(solution)/shard_map/pallas_call | solution.py:202
  173.5 2.1 collective-permute-start.18
  175.7 4.6 %shard_map.125 = bf16[4,512,256]{2,1,0:T(8,128)(2,1)S(1)} custom-call(s32[4]{0:T(128)S(1)} %get-tuple-element.45.which_ref, s32[4]{0:T(128)S(1)} %get-tuple-element.46.block_ref, bf16[256,896]{1,0:T(8,128)(2,1)S(1)} %get-tuple-element.30.g0_ref.g0, bf16[256,896]{1,0:T(8,128)(2,1)S(1)} %get-tuple-element.31.g1_ref.g2, bf16[4,256,896]{2,1,0:T(8,128)(2,1)} %bitcast.16.refs_0_, ...), custom_call_target="tpu_custom_call" | custom-call | flops 939524096 | bytes 4200000 | tf_op jit(solution)/shard_map/pallas_call | solution.py:202
  180.3 8.7 %collective-permute-done.20 = bf16[4,512,256]{2,1,0:T(8,128)(2,1)} collective-permute-done((bf16[4,512,256]{2,1,0:T(8,128)(2,1)}, bf16[4,512,256]{2,1,0:T(8,128)(2,1)}, u32[]{:S(2)}, u32[]{:S(2)}) %collective-permute-start.20) | collective-permute-done | bytes 1048608 | tf_op jit(solution)/shard_map/ppermute | solution.py:32
  189.0 9.7 %collective-permute-done.18 = bf16[4,512,256]{2,1,0:T(8,128)(2,1)} collective-permute-done((bf16[4,512,256]{2,1,0:T(8,128)(2,1)}, bf16[4,512,256]{2,1,0:T(8,128)(2,1)}, u32[]{:S(2)}, u32[]{:S(2)}) %collective-permute-start.18) | collective-permute-done | bytes 1048608 | tf_op jit(solution)/shard_map/ppermute | solution.py:32
  198.7 1.2 fusion.7
  199.9 17.4 %collective-permute-start.21 = (bf16[256,256]{1,0:T(8,128)(2,1)S(1)}, bf16[256,256]{1,0:T(8,128)(2,1)S(1)}, u32[]{:S(2)}, u32[]{:S(2)}) collective-permute-start(bf16[256,256]{1,0:T(8,128)(2,1)S(1)} %get-tuple-element.39), channel_id=1, source_target_pairs={{0,4},{1,5},{2,6},{3,7},{4,8},{5,9},{6,10},{7,11},{8,12},{9,13},{1... | collective-permute-start | bytes 393224 | tf_op jit(solution)/shard_map/ppermute | solution.py:36
  217.3 2.5 collective-permute-done.21
  219.8 1.1 fusion.4
  220.9 2.5 collective-permute-start.22
  223.4 5.6 %collective-permute-start.14 = (bf16[256,512]{1,0:T(8,128)(2,1)S(1)}, bf16[256,512]{1,0:T(8,128)(2,1)S(1)}, u32[]{:S(2)}, u32[]{:S(2)}) collective-permute-start(bf16[256,512]{1,0:T(8,128)(2,1)S(1)} %copy-done.25), channel_id=1, source_target_pairs={{0,128},{128,0},{1,129},{129,1},{2,130},{130,2},{3,131},{131,3},{4... | collective-permute-start | bytes 786440 | tf_op jit(solution)/shard_map/ppermute | solution.py:28
  229.0 3.2 %collective-permute-done.22 = bf16[256,256]{1,0:T(8,128)(2,1)S(1)} collective-permute-done((bf16[256,256]{1,0:T(8,128)(2,1)S(1)}, bf16[256,256]{1,0:T(8,128)(2,1)S(1)}, u32[]{:S(2)}, u32[]{:S(2)}) %collective-permute-start.22) | collective-permute-done | bytes 131104 | tf_op jit(solution)/shard_map/ppermute | solution.py:36
  232.2 1.3 fusion.3
  233.7 3.2 %collective-permute-start.26 = (bf16[256,256]{1,0:T(8,128)(2,1)S(1)}, bf16[256,256]{1,0:T(8,128)(2,1)S(1)}, u32[]{:S(2)}, u32[]{:S(2)}) collective-permute-start(bf16[256,256]{1,0:T(8,128)(2,1)S(1)} %get-tuple-element.38), channel_id=1, source_target_pairs={{0,140},{1,141},{2,142},{3,143},{4,0},{5,1},{6,2},{7,3},{8,4},{9,5... | collective-permute-start | bytes 393224 | tf_op jit(solution)/shard_map/ppermute | solution.py:36
  236.9 5.3 %collective-permute-done.14 = bf16[256,512]{1,0:T(8,128)(2,1)S(1)} collective-permute-done((bf16[256,512]{1,0:T(8,128)(2,1)S(1)}, bf16[256,512]{1,0:T(8,128)(2,1)S(1)}, u32[]{:S(2)}, u32[]{:S(2)}) %collective-permute-start.14) | collective-permute-done | bytes 262176 | tf_op jit(solution)/shard_map/ppermute | solution.py:28
  243.0 2.0 fusion.2
  245.1 1.2 collective-permute-start.27
  247.1 14.8 %collective-permute-start.30 = (bf16[256,896]{1,0:T(8,128)(2,1)}, bf16[256,896]{1,0:T(8,128)(2,1)S(1)}, u32[]{:S(2)}, u32[]{:S(2)}) collective-permute-start(bf16[256,896]{1,0:T(8,128)(2,1)} %reduce-scatter.5.cloned.1.call-done), channel_id=1, source_target_pairs={{0,128},{128,0},{1,129},{129,1},{2,130},{130,2},{3,131},{131,3},{4... | collective-permute-start | bytes 1376264 | tf_op jit(solution)/shard_map/ppermute | solution.py:28
  264.8 1.9 fusion.6
  266.7 8.3 %collective-permute-done.30.recv_ref = bf16[256,896]{1,0:T(8,128)(2,1)S(1)} collective-permute-done((bf16[256,896]{1,0:T(8,128)(2,1)}, bf16[256,896]{1,0:T(8,128)(2,1)S(1)}, u32[]{:S(2)}, u32[]{:S(2)}) %collective-permute-start.30) | collective-permute-done | bytes 458784 | tf_op jit(solution)/shard_map/ppermute | solution.py:28
  275.0 1.2 copy-done.14
  276.2 1.0 copy-done.18
  277.2 4.1 %shard_map.132 = (f32[256,1792]{1,0:T(8,128)}, bf16[256,1792]{1,0:T(8,128)(2,1)}, bf16[256,1792]{1,0:T(8,128)(2,1)}) custom-call(s32[1]{0:T(128)} %bitcast.11.opt_ref.half_ref, bf16[256,896]{1,0:T(8,128)(2,1)S(1)} %copy-done.18, bf16[256,896]{1,0:T(8,128)(2,1)S(1)} %collective-permute-done.30.recv_ref, f32[256,1792]{1,0:T(8,128)S(1)} %copy-done.6, ...), custom_call_target="tpu_custom_call" | custom-call | flops 7340032 | bytes 9437184 | tf_op jit(solution)/shard_map/pallas_call | solution.py:279
  (118 shorter events, 17.2 us)
Async XLA Ops:
  7.2 81.8 %all-gather.2.cloned.1.call-start = ((), (), s32[]{:S(2)}) async-start(), calls=%async_computation.2 | async-start | bytes 2359296 | tf_op jit(solution)/shard_map/all_gather | solution.py:321
  7.2 1.6 copy-start.3
  11.9 3.0 %collective-permute-start = (bf16[256,2048]{1,0:T(8,128)(2,1)}, bf16[256,2048]{1,0:T(8,128)(2,1)}, u32[]{:S(2)}, u32[]{:S(2)}) collective-permute-start(bf16[256,2048]{1,0:T(8,128)(2,1)} %get-tuple-element.21), channel_id=1, source_target_pairs={{0,16},{16,0},{32,48},{48,32},{64,80},{80,64},{96,112},{112,96},{1... | collective-permute-start | bytes 3145736 | tf_op jit(solution)/shard_map/ppermute | solution.py:24
  12.0 20.0 %copy-start.17 = (bf16[2,128,1792]{2,1,0:T(8,128)(2,1)S(1)}, bf16[2,128,1792]{2,1,0:T(8,128)(2,1)}, u32[]{:S(2)}) copy-start(bf16[2,128,1792]{2,1,0:T(8,128)(2,1)} %code_ref.1) | copy-start | bytes 2752516
  12.0 20.0 %copy-start.23 = (f32[2,14]{1,0:T(2,128)S(1)}, f32[2,14]{1,0:T(2,128)}, u32[]{:S(2)}) copy-start(f32[2,14]{1,0:T(2,128)} %scale_ref.1) | copy-start | bytes 340
  16.2 55.8 %copy-start = (bf16[512,2048]{1,0:T(8,128)(2,1)}, bf16[512,2048]{1,0:T(8,128)(2,1)S(1)}, u32[]{:S(2)}) copy-start(bf16[512,2048]{1,0:T(8,128)(2,1)S(1)} %constant_dynamic-update-slice_fusion.tok_ref.t0_ref) | copy-start | bytes 6291460
  16.2 15.0 %collective-permute-start.11 = (bf16[64,2048]{1,0:T(8,128)(2,1)S(1)}, bf16[64,2048]{1,0:T(8,128)(2,1)S(1)}, u32[]{:S(2)}, u32[]{:S(2)}) collective-permute-start(bf16[64,2048]{1,0:T(8,128)(2,1)S(1)} %constant_dynamic-slice_fusion), channel_id=1, source_target_pairs={{0,128},{128,0},{1,129},{129,1},{2,130},{130,2},{3,131},{131,3},{4... | collective-permute-start | bytes 786440 | tf_op jit(solution)/shard_map/ppermute | solution.py:28
  31.2 0.7 copy-start.27
  31.9 215.2 %reduce-scatter.5.cloned.1.call-start = ((), (), s32[]{:S(2)}) async-start(), calls=%async_computation.4 | async-start | bytes 2293760 | tf_op jit(solution)/shard_map/reduce_scatter | solution.py:388
  33.6 25.2 %collective-permute-start.5 = (bf16[256,896]{1,0:T(8,128)(2,1)S(1)}, bf16[256,896]{1,0:T(8,128)(2,1)}, u32[]{:S(2)}, u32[]{:S(2)}) collective-permute-start(bf16[256,896]{1,0:T(8,128)(2,1)S(1)} %get-tuple-element.23), channel_id=1, source_target_pairs={{0,128},{128,0},{1,129},{129,1},{2,130},{130,2},{3,131},{131,3},{4... | collective-permute-start | bytes 1376264 | tf_op jit(solution)/shard_map/ppermute | solution.py:28
  43.1 17.8 %collective-permute-start.1 = (bf16[256,896]{1,0:T(8,128)(2,1)}, bf16[256,896]{1,0:T(8,128)(2,1)}, u32[]{:S(2)}, u32[]{:S(2)}) collective-permute-start(bf16[256,896]{1,0:T(8,128)(2,1)} %get-tuple-element.22.refs_0_), channel_id=1, source_target_pairs={{0,32},{16,48},{32,64},{48,80},{64,96},{80,112},{96,0},{112,16},{1... | collective-permute-start | bytes 1376264 | tf_op jit(solution)/shard_map/ppermute | solution.py:20
  43.6 20.7 %collective-permute-start.2 = (bf16[256,896]{1,0:T(8,128)(2,1)}, bf16[256,896]{1,0:T(8,128)(2,1)}, u32[]{:S(2)}, u32[]{:S(2)}) collective-permute-start(bf16[256,896]{1,0:T(8,128)(2,1)} %get-tuple-element.22.refs_0_), channel_id=1, source_target_pairs={{0,96},{16,112},{32,0},{48,16},{64,32},{80,48},{96,64},{112,80},{1... | collective-permute-start | bytes 1376264 | tf_op jit(solution)/shard_map/ppermute | solution.py:20
  58.9 9.0 %collective-permute-start.6 = (bf16[256,896]{1,0:T(8,128)(2,1)}, bf16[256,896]{1,0:T(8,128)(2,1)S(1)}, u32[]{:S(2)}, u32[]{:S(2)}) collective-permute-start(bf16[256,896]{1,0:T(8,128)(2,1)} %collective-permute-done.5.refs_5_), channel_id=1, source_target_pairs={{0,32},{16,48},{32,64},{48,80},{64,96},{80,112},{96,0},{112,16},{1... | collective-permute-start | bytes 1376264 | tf_op jit(solution)/shard_map/ppermute | solution.py:20
  59.4 11.8 %collective-permute-start.7 = (bf16[256,896]{1,0:T(8,128)(2,1)}, bf16[256,896]{1,0:T(8,128)(2,1)S(1)}, u32[]{:S(2)}, u32[]{:S(2)}) collective-permute-start(bf16[256,896]{1,0:T(8,128)(2,1)} %collective-permute-done.5.refs_5_), channel_id=1, source_target_pairs={{0,96},{16,112},{32,0},{48,16},{64,32},{80,48},{96,64},{112,80},{1... | collective-permute-start | bytes 1376264 | tf_op jit(solution)/shard_map/ppermute | solution.py:20
  62.5 11.1 %collective-permute-start.3 = (bf16[128,896]{1,0:T(8,128)(2,1)}, bf16[128,896]{1,0:T(8,128)(2,1)S(1)}, u32[]{:S(2)}, u32[]{:S(2)}) collective-permute-start(bf16[128,896]{1,0:T(8,128)(2,1)} %slice.56), channel_id=1, source_target_pairs={{0,32},{16,48},{32,64},{48,80},{64,96},{80,112},{96,0},{112,16},{1... | collective-permute-start | bytes 688136 | tf_op jit(solution)/shard_map/ppermute | solution.py:20
  65.9 7.7 %collective-permute-start.4 = (bf16[128,896]{1,0:T(8,128)(2,1)}, bf16[128,896]{1,0:T(8,128)(2,1)}, u32[]{:S(2)}, u32[]{:S(2)}) collective-permute-start(bf16[128,896]{1,0:T(8,128)(2,1)} %slice.57), channel_id=1, source_target_pairs={{0,96},{16,112},{32,0},{48,16},{64,32},{80,48},{96,64},{112,80},{1... | collective-permute-start | bytes 688136 | tf_op jit(solution)/shard_map/ppermute | solution.py:20
  67.9 21.1 %copy-start.9 = (bf16[256,896]{1,0:T(8,128)(2,1)}, bf16[256,896]{1,0:T(8,128)(2,1)S(1)}, u32[]{:S(2)}) copy-start(bf16[256,896]{1,0:T(8,128)(2,1)S(1)} %collective-permute-done.6.refs_6_) | copy-start | bytes 1376260
  68.7 6.4 %collective-permute-start.8 = (bf16[128,896]{1,0:T(8,128)(2,1)}, bf16[128,896]{1,0:T(8,128)(2,1)S(1)}, u32[]{:S(2)}, u32[]{:S(2)}) collective-permute-start(bf16[128,896]{1,0:T(8,128)(2,1)} %slice.58), channel_id=1, source_target_pairs={{0,32},{16,48},{32,64},{48,80},{64,96},{80,112},{96,0},{112,16},{1... | collective-permute-start | bytes 688136 | tf_op jit(solution)/shard_map/ppermute | solution.py:20
  71.2 17.8 %copy-start.11 = (bf16[256,896]{1,0:T(8,128)(2,1)}, bf16[256,896]{1,0:T(8,128)(2,1)S(1)}, u32[]{:S(2)}) copy-start(bf16[256,896]{1,0:T(8,128)(2,1)S(1)} %collective-permute-done.7.refs_7_) | copy-start | bytes 1376260
  71.9 7.5 %collective-permute-start.9 = (bf16[128,896]{1,0:T(8,128)(2,1)}, bf16[128,896]{1,0:T(8,128)(2,1)}, u32[]{:S(2)}, u32[]{:S(2)}) collective-permute-start(bf16[128,896]{1,0:T(8,128)(2,1)} %slice.59), channel_id=1, source_target_pairs={{0,96},{16,112},{32,0},{48,16},{64,32},{80,48},{96,64},{112,80},{1... | collective-permute-start | bytes 688136 | tf_op jit(solution)/shard_map/ppermute | solution.py:20
  73.6 15.4 %copy-start.19 = (bf16[128,896]{1,0:T(8,128)(2,1)}, bf16[128,896]{1,0:T(8,128)(2,1)S(1)}, u32[]{:S(2)}) copy-start(bf16[128,896]{1,0:T(8,128)(2,1)S(1)} %collective-permute-done.3.refs_3_) | copy-start | bytes 688132
  75.0 13.9 %copy-start.21 = (bf16[128,896]{1,0:T(8,128)(2,1)}, bf16[128,896]{1,0:T(8,128)(2,1)S(1)}, u32[]{:S(2)}) copy-start(bf16[128,896]{1,0:T(8,128)(2,1)S(1)} %collective-permute-done.8.refs_8_) | copy-start | bytes 688132
  84.5 0.9 copy-start.15
  85.4 8.7 %slice-start.1 = ((bf16[256,896]{1,0:T(8,128)(2,1)}), bf16[256,384]{1,0:T(8,128)(2,1)S(1)}, s32[]{:S(2)}) async-start(bf16[256,896]{1,0:T(8,128)(2,1)} %param.9), calls=%async_computation.6 | async-start | bytes 393216 | tf_op jit(solution)/shard_map/slice | solution.py:324
  85.4 12.4 %collective-permute-start.10 = (bf16[256,896]{1,0:T(8,128)(2,1)S(1)}, bf16[256,896]{1,0:T(8,128)(2,1)S(1)}, u32[]{:S(2)}, u32[]{:S(2)}) collective-permute-start(bf16[256,896]{1,0:T(8,128)(2,1)S(1)} %get-tuple-element.25), channel_id=1, source_target_pairs={{0,16},{16,0},{32,48},{48,32},{64,80},{80,64},{96,112},{112,96},{1... | collective-permute-start | bytes 1376264 | tf_op jit(solution)/shard_map/ppermute | solution.py:24
  89.0 8.9 %copy-start.16 = (f32[256,896]{1,0:T(8,128)S(1)}, f32[256,896]{1,0:T(8,128)}, u32[]{:S(2)}) copy-start(f32[256,896]{1,0:T(8,128)} %copy-done.15) | copy-start | bytes 2752516
  94.0 14.0 %collective-permute-start.12 = (bf16[256,896]{1,0:T(8,128)(2,1)S(1)}, bf16[256,896]{1,0:T(8,128)(2,1)S(1)}, u32[]{:S(2)}, u32[]{:S(2)}) collective-permute-start(bf16[256,896]{1,0:T(8,128)(2,1)S(1)} %get-tuple-element.28), channel_id=1, source_target_pairs={{0,16},{16,0},{32,48},{48,32},{64,80},{80,64},{96,112},{112,96},{1... | collective-permute-start | bytes 1376264 | tf_op jit(solution)/shard_map/ppermute | solution.py:24
  95.2 15.8 %copy-start.1 = (bf16[512,2048]{1,0:T(8,128)(2,1)S(1)}, bf16[512,2048]{1,0:T(8,128)(2,1)}, u32[]{:S(2)}) copy-start(bf16[512,2048]{1,0:T(8,128)(2,1)} %copy-done) | copy-start | bytes 6291460
  95.2 12.8 %collective-permute-start.13 = (bf16[256,512]{1,0:T(8,128)(2,1)S(1)}, bf16[256,512]{1,0:T(8,128)(2,1)S(1)}, u32[]{:S(2)}, u32[]{:S(2)}) collective-permute-start(bf16[256,512]{1,0:T(8,128)(2,1)S(1)} %get-tuple-element.42), channel_id=1, source_target_pairs={{0,128},{128,0},{1,129},{129,1},{2,130},{130,2},{3,131},{131,3},{4... | collective-permute-start | bytes 786440 | tf_op jit(solution)/shard_map/ppermute | solution.py:28
  98.4 10.9 %collective-permute-start.28 = (bf16[256,896]{1,0:T(8,128)(2,1)S(1)}, bf16[256,896]{1,0:T(8,128)(2,1)S(1)}, u32[]{:S(2)}, u32[]{:S(2)}) collective-permute-start(bf16[256,896]{1,0:T(8,128)(2,1)S(1)} %get-tuple-element.30.g0_ref.g0), channel_id=1, source_target_pairs={{0,16},{16,0},{32,48},{48,32},{64,80},{80,64},{96,112},{112,96},{1... | collective-permute-start | bytes 1376264 | tf_op jit(solution)/shard_map/ppermute | solution.py:24
  108.5 0.7 copy-start.24
  109.2 1.8 collective-permute-start.29
  116.2 0.8 copy-start.7
  117.1 149.6 %reduce-scatter.3.cloned.1.call-start = ((), (), s32[]{:S(2)}) async-start(), calls=%async_computation.3 | async-start | bytes 2293760 | tf_op jit(solution)/shard_map/reduce_scatter | solution.py:391
  117.1 6.7 %copy-start.20 = (bf16[128,896]{1,0:T(8,128)(2,1)S(1)}, bf16[128,896]{1,0:T(8,128)(2,1)}, u32[]{:S(2)}) copy-start(bf16[128,896]{1,0:T(8,128)(2,1)} %copy-done.19) | copy-start | bytes 688132
  119.0 7.4 %copy-start.10 = (bf16[256,896]{1,0:T(8,128)(2,1)S(1)}, bf16[256,896]{1,0:T(8,128)(2,1)}, u32[]{:S(2)}) copy-start(bf16[256,896]{1,0:T(8,128)(2,1)} %copy-done.9) | copy-start | bytes 1376260
  120.1 6.3 %copy-start.12 = (bf16[256,896]{1,0:T(8,128)(2,1)S(1)}, bf16[256,896]{1,0:T(8,128)(2,1)}, u32[]{:S(2)}) copy-start(bf16[256,896]{1,0:T(8,128)(2,1)} %copy-done.11) | copy-start | bytes 1376260
  122.0 4.5 %copy-start.22 = (bf16[128,896]{1,0:T(8,128)(2,1)S(1)}, bf16[128,896]{1,0:T(8,128)(2,1)}, u32[]{:S(2)}) copy-start(bf16[128,896]{1,0:T(8,128)(2,1)} %copy-done.21) | copy-start | bytes 688132
  126.2 4.1 %collective-permute-start.15 = (bf16[1024,896]{1,0:T(8,128)(2,1)}, bf16[1024,896]{1,0:T(8,128)(2,1)}, u32[]{:S(2)}, u32[]{:S(2)}) collective-permute-start(bf16[1024,896]{1,0:T(8,128)(2,1)} %constant_dynamic-update-slice_fusion.2), channel_id=1, source_target_pairs={{0,16},{16,0},{32,48},{48,32},{64,80},{80,64},{96,112},{112,96},{1... | collective-permute-start | bytes 5505032 | tf_op jit(solution)/shard_map/ppermute | solution.py:24
  127.5 5.3 %collective-permute-start.16 = (bf16[1024,896]{1,0:T(8,128)(2,1)S(1)}, bf16[1024,896]{1,0:T(8,128)(2,1)}, u32[]{:S(2)}, u32[]{:S(2)}) collective-permute-start(bf16[1024,896]{1,0:T(8,128)(2,1)S(1)} %constant_dynamic-update-slice_fusion.7), channel_id=1, source_target_pairs={{0,16},{16,0},{32,48},{48,32},{64,80},{80,64},{96,112},{112,96},{1... | collective-permute-start | bytes 5505032 | tf_op jit(solution)/shard_map/ppermute | solution.py:24
  132.8 3.8 %copy-start.2 = (bf16[512,2048]{1,0:T(8,128)(2,1)S(1)}, bf16[512,2048]{1,0:T(8,128)(2,1)}, u32[]{:S(2)}) copy-start(bf16[512,2048]{1,0:T(8,128)(2,1)} %copy-done) | copy-start | bytes 6291460
  132.8 3.8 %copy-start.8 = (bf16[256,896]{1,0:T(8,128)(2,1)S(1)}, bf16[256,896]{1,0:T(8,128)(2,1)}, u32[]{:S(2)}) copy-start(bf16[256,896]{1,0:T(8,128)(2,1)} %copy-done.7) | copy-start | bytes 1376260
  136.6 22.0 %collective-permute-start.19 = (bf16[2,512,256]{2,1,0:T(8,128)(2,1)}, bf16[2,512,256]{2,1,0:T(8,128)(2,1)}, u32[]{:S(2)}, u32[]{:S(2)}) collective-permute-start(bf16[2,512,256]{2,1,0:T(8,128)(2,1)} %shard_map.128), channel_id=1, source_target_pairs={{0,3},{1,0},{2,1},{3,2},{4,7},{5,4},{6,5},{7,6},{8,11},{9,8},{10,9... | collective-permute-start | bytes 1572872 | tf_op jit(solution)/shard_map/ppermute | solution.py:32
  140.9 1.2 copy-start.4
  145.2 23.5 %collective-permute-start.17 = (bf16[2,512,256]{2,1,0:T(8,128)(2,1)S(1)}, bf16[2,512,256]{2,1,0:T(8,128)(2,1)}, u32[]{:S(2)}, u32[]{:S(2)}) collective-permute-start(bf16[2,512,256]{2,1,0:T(8,128)(2,1)S(1)} %shard_map.126), channel_id=1, source_target_pairs={{0,1},{1,2},{2,3},{3,0},{4,5},{5,6},{6,7},{7,4},{8,9},{9,10},{10,1... | collective-permute-start | bytes 1572872 | tf_op jit(solution)/shard_map/ppermute | solution.py:32
  164.0 25.0 %collective-permute-start.20 = (bf16[4,512,256]{2,1,0:T(8,128)(2,1)}, bf16[4,512,256]{2,1,0:T(8,128)(2,1)}, u32[]{:S(2)}, u32[]{:S(2)}) collective-permute-start(bf16[4,512,256]{2,1,0:T(8,128)(2,1)} %shard_map.129), channel_id=1, source_target_pairs={{0,3},{1,0},{2,1},{3,2},{4,7},{5,4},{6,5},{7,6},{8,11},{9,8},{10,9... | collective-permute-start | bytes 3145736 | tf_op jit(solution)/shard_map/ppermute | solution.py:32
  173.5 25.2 %collective-permute-start.18 = (bf16[4,512,256]{2,1,0:T(8,128)(2,1)}, bf16[4,512,256]{2,1,0:T(8,128)(2,1)}, u32[]{:S(2)}, u32[]{:S(2)}) collective-permute-start(bf16[4,512,256]{2,1,0:T(8,128)(2,1)} %shard_map.127), channel_id=1, source_target_pairs={{0,1},{1,2},{2,3},{3,0},{4,5},{5,6},{6,7},{7,4},{8,9},{9,10},{10,1... | collective-permute-start | bytes 3145736 | tf_op jit(solution)/shard_map/ppermute | solution.py:32
  175.7 47.7 %copy-start.25 = (bf16[256,512]{1,0:T(8,128)(2,1)S(1)}, bf16[256,512]{1,0:T(8,128)(2,1)}, u32[]{:S(2)}) copy-start(bf16[256,512]{1,0:T(8,128)(2,1)} %copy-done.24) | copy-start | bytes 786436
  180.3 18.4 %copy-start.5 = (bf16[4,512,256]{2,1,0:T(8,128)(2,1)}, bf16[4,512,256]{2,1,0:T(8,128)(2,1)S(1)}, u32[]{:S(2)}) copy-start(bf16[4,512,256]{2,1,0:T(8,128)(2,1)S(1)} %shard_map.125) | copy-start | bytes 3145732
  199.9 19.9 %collective-permute-start.21 = (bf16[256,256]{1,0:T(8,128)(2,1)S(1)}, bf16[256,256]{1,0:T(8,128)(2,1)S(1)}, u32[]{:S(2)}, u32[]{:S(2)}) collective-permute-start(bf16[256,256]{1,0:T(8,128)(2,1)S(1)} %get-tuple-element.39), channel_id=1, source_target_pairs={{0,4},{1,5},{2,6},{3,7},{4,8},{5,9},{6,10},{7,11},{8,12},{9,13},{1... | collective-permute-start | bytes 393224 | tf_op jit(solution)/shard_map/ppermute | solution.py:36
  217.3 11.8 %collective-permute-start.25 = (bf16[256,256]{1,0:T(8,128)(2,1)S(1)}, bf16[256,256]{1,0:T(8,128)(2,1)S(1)}, u32[]{:S(2)}, u32[]{:S(2)}) collective-permute-start(bf16[256,256]{1,0:T(8,128)(2,1)S(1)} %get-tuple-element.40), channel_id=1, source_target_pairs={{0,140},{1,141},{2,142},{3,143},{4,0},{5,1},{6,2},{7,3},{8,4},{9,5... | collective-permute-start | bytes 393224 | tf_op jit(solution)/shard_map/ppermute | solution.py:36
  220.9 11.4 %collective-permute-start.22 = (bf16[256,256]{1,0:T(8,128)(2,1)S(1)}, bf16[256,256]{1,0:T(8,128)(2,1)S(1)}, u32[]{:S(2)}, u32[]{:S(2)}) collective-permute-start(bf16[256,256]{1,0:T(8,128)(2,1)S(1)} %fusion.4), channel_id=1, source_target_pairs={{0,4},{1,5},{2,6},{3,7},{4,8},{5,9},{6,10},{7,11},{8,12},{9,13},{1... | collective-permute-start | bytes 393224 | tf_op jit(solution)/shard_map/ppermute | solution.py:36
  223.4 18.8 %collective-permute-start.14 = (bf16[256,512]{1,0:T(8,128)(2,1)S(1)}, bf16[256,512]{1,0:T(8,128)(2,1)S(1)}, u32[]{:S(2)}, u32[]{:S(2)}) collective-permute-start(bf16[256,512]{1,0:T(8,128)(2,1)S(1)} %copy-done.25), channel_id=1, source_target_pairs={{0,128},{128,0},{1,129},{129,1},{2,130},{130,2},{3,131},{131,3},{4... | collective-permute-start | bytes 786440 | tf_op jit(solution)/shard_map/ppermute | solution.py:28
  233.6 9.4 %collective-permute-start.23 = (bf16[256,256]{1,0:T(8,128)(2,1)S(1)}, bf16[256,256]{1,0:T(8,128)(2,1)S(1)}, u32[]{:S(2)}, u32[]{:S(2)}) collective-permute-start(bf16[256,256]{1,0:T(8,128)(2,1)S(1)} %get-tuple-element.37), channel_id=1, source_target_pairs={{0,4},{1,5},{2,6},{3,7},{4,8},{5,9},{6,10},{7,11},{8,12},{9,13},{1... | collective-permute-start | bytes 393224 | tf_op jit(solution)/shard_map/ppermute | solution.py:36
  233.7 9.3 %collective-permute-start.26 = (bf16[256,256]{1,0:T(8,128)(2,1)S(1)}, bf16[256,256]{1,0:T(8,128)(2,1)S(1)}, u32[]{:S(2)}, u32[]{:S(2)}) collective-permute-start(bf16[256,256]{1,0:T(8,128)(2,1)S(1)} %get-tuple-element.38), channel_id=1, source_target_pairs={{0,140},{1,141},{2,142},{3,143},{4,0},{5,1},{6,2},{7,3},{8,4},{9,5... | collective-permute-start | bytes 393224 | tf_op jit(solution)/shard_map/ppermute | solution.py:36
  242.2 0.8 copy-start.26
  243.0 20.9 %slice-start = ((bf16[256,512]{1,0:T(8,128)(2,1)}), bf16[256,64]{1,0:T(8,128)(2,1)S(1)}, s32[]{:S(2)}) async-start(bf16[256,512]{1,0:T(8,128)(2,1)} %broadcast_select_fusion), calls=%async_computation.5 | async-start | bytes 131072 | tf_op jit(solution)/shard_map/slice | solution.py:341
  245.1 29.9 %copy-start.6 = (f32[256,1792]{1,0:T(8,128)S(1)}, f32[256,1792]{1,0:T(8,128)}, u32[]{:S(2)}) copy-start(f32[256,1792]{1,0:T(8,128)} %master_ref.1) | copy-start | bytes 5505028
  245.1 29.9 %copy-start.13 = (bf16[256,1792]{1,0:T(8,128)(2,1)S(1)}, bf16[256,1792]{1,0:T(8,128)(2,1)}, u32[]{:S(2)}) copy-start(bf16[256,1792]{1,0:T(8,128)(2,1)} %m_ref.1) | copy-start | bytes 2752516
  245.1 19.7 %collective-permute-start.27 = (bf16[256,256]{1,0:T(8,128)(2,1)}, bf16[256,256]{1,0:T(8,128)(2,1)}, u32[]{:S(2)}, u32[]{:S(2)}) collective-permute-start(bf16[256,256]{1,0:T(8,128)(2,1)} %get-tuple-element.36), channel_id=1, source_target_pairs={{0,140},{1,141},{2,142},{3,143},{4,0},{5,1},{6,2},{7,3},{8,4},{9,5... | collective-permute-start | bytes 393224 | tf_op jit(solution)/shard_map/ppermute | solution.py:36
  246.2 18.6 %collective-permute-start.24 = (bf16[256,256]{1,0:T(8,128)(2,1)}, bf16[256,256]{1,0:T(8,128)(2,1)}, u32[]{:S(2)}, u32[]{:S(2)}) collective-permute-start(bf16[256,256]{1,0:T(8,128)(2,1)} %get-tuple-element.35), channel_id=1, source_target_pairs={{0,4},{1,5},{2,6},{3,7},{4,8},{5,9},{6,10},{7,11},{8,12},{9,13},{1... | collective-permute-start | bytes 393224 | tf_op jit(solution)/shard_map/ppermute | solution.py:36
  247.1 27.8 %collective-permute-start.30 = (bf16[256,896]{1,0:T(8,128)(2,1)}, bf16[256,896]{1,0:T(8,128)(2,1)S(1)}, u32[]{:S(2)}, u32[]{:S(2)}) collective-permute-start(bf16[256,896]{1,0:T(8,128)(2,1)} %reduce-scatter.5.cloned.1.call-done), channel_id=1, source_target_pairs={{0,128},{128,0},{1,129},{129,1},{2,130},{130,2},{3,131},{131,3},{4... | collective-permute-start | bytes 1376264 | tf_op jit(solution)/shard_map/ppermute | solution.py:28
  275.0 1.2 copy-start.14
  276.2 1.0 copy-start.18
Sparse Core Ops, SparseCore 0:
  32.1 56.8 all-gather.1
  117.2 42.8 reduce-scatter.4
  162.6 29.8 reduce-scatter.2

commit v2 on v1

v2 whole, which is shorter than its diff:
```python
import functools

import jax
import jax.numpy as jnp
from jax import lax
from jax.experimental import pallas as pl
from jax.experimental.pallas import tpu as pltpu
from jax.sharding import PartitionSpec as P

F32 = jnp.float32
BF16 = jnp.bfloat16
OT = ("opt", "tensor")
VMEM = pl.BlockSpec(memory_space=pltpu.VMEM)
SMEM = pl.BlockSpec(memory_space=pltpu.SMEM)
LIMIT = 28 * 1024 * 1024
COST = pl.CostEstimate(flops=1, bytes_accessed=1 << 20, transcendentals=0)


X_GROUPS = [[0, 2, 4, 6], [1, 3, 5, 7]]
EIGHTHS = [list(range(8)), list(range(8, 16))]


def along_x(a, step):
    return lax.ppermute(a, "dp", [(x * 2 + c, (x + step) % 4 * 2 + c) for x in range(4) for c in range(2)])


def other_core(a):
    return lax.ppermute(a, "dp", [(i, i ^ 1) for i in range(8)])


def other_opt(a):
    return lax.ppermute(a, "opt", [(0, 1), (1, 0)])


def along_y(a, step):
    return lax.ppermute(a, "tensor", [(z * 4 + y, z * 4 + (y + step) % 4) for z in range(4) for y in range(4)])


def along_z(a, step):
    return lax.ppermute(a, OT, [(z * 4 + y, (z + step) % 8 * 4 + y) for z in range(8) for y in range(4)])


def params(limit=LIMIT):
    return pltpu.CompilerParams(vmem_limit_bytes=limit)


def low_lanes(shape):
    return lax.broadcasted_iota(jnp.int32, shape, 1) < 64


def prepare_kernel(opt_ref, scale_ref, code_ref, own_ref, send_ref):
    first = opt_ref[0] == 0
    low = low_lanes((128, 128))

    def put(rows, at, half0, half1):
        own_ref[rows, at : at + 128] = jnp.where(first, half0, half1).astype(BF16)
        send_ref[rows, at : at + 128] = jnp.where(first, half1, half0).astype(BF16)

    for b in range(2):
        rows = slice(b * 128, b * 128 + 128)

        def tile(j):
            return code_ref[b, :, j * 128 : j * 128 + 128].astype(F32) * scale_ref[b, j]

        for part in range(2):
            for j in range(3):
                put(rows, part * 384 + j * 128, tile(part * 7 + j), tile(part * 7 + 4 + j))
        gate, up = tile(3), tile(10)
        put(
            rows,
            768,
            jnp.where(low, gate, pltpu.roll(up, 64, 1)),
            jnp.where(low, pltpu.roll(gate, 64, 1), up),
        )


def prepare(opt, scales, codes):
    out = jax.ShapeDtypeStruct((256, 896), BF16)
    return pl.pallas_call(
        prepare_kernel,
        out_shape=(out, out),
        in_specs=[SMEM, SMEM, VMEM],
        out_specs=(VMEM, VMEM),
        compiler_params=params(),
        cost_estimate=COST,
    )(opt, scales, codes)


def split_kernel(core_ref, keep_in, send_in, keep_ref, send_ref):
    keep_ref[...] = keep_in[...]
    send_ref[...] = send_in[...]


def split_tokens(core, tokens):
    rows = tokens.shape[0]
    out = jax.ShapeDtypeStruct((rows, 2048), BF16)

    def block(column):
        return pl.BlockSpec((rows, 256), lambda i, core: (0, column(i, core[0])))

    return pl.pallas_call(
        split_kernel,
        out_shape=(out, out),
        grid_spec=pltpu.PrefetchScalarGridSpec(
            num_scalar_prefetch=1,
            grid=(8,),
            in_specs=[block(lambda i, c: 2 * i + c), block(lambda i, c: 2 * i + 1 - c)],
            out_specs=(block(lambda i, c: i), block(lambda i, c: i)),
        ),
        compiler_params=params(),
        cost_estimate=COST,
    )(core, tokens, tokens)


def joined_kernel(out_ref, pieces):
    for i, piece in enumerate(pieces):
        out_ref[i] = piece[...]


def near_kernel(at_ref, r0_ref, r1_ref, *refs):
    pieces, (total_ref, joined_ref) = refs[:-2], refs[-2:]
    joined_kernel(joined_ref, pieces)
    for half, tok in enumerate((r0_ref, r1_ref)):
        total = None
        for i in range(4):
            columns = pl.ds(pl.multiple_of(at_ref[i] * 256, 256), 256)
            term = jnp.dot(tok[:, columns], joined_ref[i], preferred_element_type=F32)
            total = term if total is None else total + term
        total_ref[half * 256 : half * 256 + 256] = total


def project_near(at, r0, r1, pieces):
    return pl.pallas_call(
        near_kernel,
        out_shape=(jax.ShapeDtypeStruct((512, 896), F32), jax.ShapeDtypeStruct((4, 256, 896), BF16)),
        in_specs=[SMEM] + [VMEM] * 6,
        out_specs=(VMEM, VMEM),
        compiler_params=params(),
        cost_estimate=COST,
    )(at, r0, r1, *pieces)


def far_kernel(at_ref, r0_ref, r1_ref, theirs_ref, total_ref, near_ref, *refs):
    pieces, (own_ref, send_ref, joined_ref) = refs[:-3], refs[-3:]
    joined_kernel(joined_ref, pieces)
    for k in range(4):
        total = total_ref[k * 256 : k * 256 + 256] if k < 2 else None
        for i in range(4 if k < 2 else 0, 8):
            columns = pl.ds(pl.multiple_of(at_ref[i] * 256, 256), 256)
            weights = near_ref if i < 4 else joined_ref
            if k < 2:
                tok = (r0_ref, r1_ref)[k][:, columns]
            else:
                tok = theirs_ref[:, k - 2, :, columns].reshape(256, 256)
            term = jnp.dot(tok, weights[i % 4], preferred_element_type=F32)
            total = term if total is None else total + term
        if k % 2 == 0:
            own_ref[k // 2] = total
        else:
            send_ref[k // 2] = total.astype(BF16)


def project_far(at, *args):
    return pl.pallas_call(
        far_kernel,
        out_shape=(
            jax.ShapeDtypeStruct((2, 256, 896), F32),
            jax.ShapeDtypeStruct((2, 256, 896), BF16),
            jax.ShapeDtypeStruct((4, 256, 896), BF16),
        ),
        in_specs=[SMEM] + [VMEM] * 9,
        out_specs=(VMEM, VMEM, VMEM),
        compiler_params=params(),
        cost_estimate=COST,
    )(at, *args)


def swiglu_kernel(*refs):
    own_ref, recv_ref, *up_grads, hidden0_ref, hidden1_ref, grad_ref = refs

    def parts(gate, up, upstream):
        s = 1.0 / (1.0 + jnp.exp(-gate))
        act = gate * s
        return act * up, upstream * up * s * (1.0 + gate * (1.0 - s)), upstream * act

    for half, (up_grad_ref, hidden_ref) in enumerate(zip(up_grads, (hidden0_ref, hidden1_ref))):

        def projected(at):
            return own_ref[half, :, at : at + 128] + recv_ref[half, :, at : at + 128].astype(F32)

        for j in range(3):
            at = j * 128
            hidden, grad_gate, grad_up = parts(
                projected(at), projected(384 + at), up_grad_ref[:, at : at + 128].astype(F32)
            )
            hidden_ref[:, at : at + 128] = hidden.astype(BF16)
            grad_ref[half, :, at : at + 128] = grad_gate.astype(BF16)
            grad_ref[half, :, 384 + at : 384 + at + 128] = grad_up.astype(BF16)
        mixed = projected(768)
        hidden, grad_gate, grad_up = parts(mixed, pltpu.roll(mixed, 64, 1), up_grad_ref[:, 384:512].astype(F32))
        hidden_ref[:, 384:512] = hidden.astype(BF16)
        grad_ref[half, :, 768:896] = jnp.where(
            low_lanes(mixed.shape), grad_gate, pltpu.roll(grad_up, 64, 1)
        ).astype(BF16)


def swiglu(*args):
    hidden = jax.ShapeDtypeStruct((256, 512), BF16)
    return pl.pallas_call(
        swiglu_kernel,
        out_shape=(hidden, hidden, jax.ShapeDtypeStruct((2, 256, 896), BF16)),
        in_specs=[VMEM] * 4,
        out_specs=(VMEM, VMEM, VMEM),
        compiler_params=params(),
        cost_estimate=COST,
    )(*args)


def token_grad_kernel(which_ref, block_ref, half_ref, g_ref, *refs):
    weights, out_refs = refs[:4], refs[4:]
    for k, out_ref in enumerate(out_refs):
        size = out_ref.shape[0]

        def step(j, _):
            i = k * size + j
            for a in range(4):

                @pl.when(which_ref[i] == a)
                def _():
                    out_ref[j] = lax.dot_general(
                        g_ref[half_ref[i]],
                        weights[a][block_ref[i]],
                        (((1,), (1,)), ((), ())),
                        preferred_element_type=F32,
                    ).astype(BF16)

            return 0

        lax.fori_loop(0, size, step, 0)


def token_grad(table, g, weights, outs):
    size = table[0].shape[0] // outs
    return pl.pallas_call(
        token_grad_kernel,
        out_shape=[jax.ShapeDtypeStruct((size, 256, 256), BF16)] * outs,
        in_specs=[SMEM] * 3 + [VMEM] * 5,
        out_specs=[VMEM] * outs,
        compiler_params=params(),
        cost_estimate=COST,
    )(*table, g, *weights)


def add_kernel(a_ref, b_ref, c_ref, d_ref, ab_ref, cd_ref):
    ab_ref[...] = (a_ref[...].astype(F32) + b_ref[...].astype(F32)).astype(BF16)
    cd_ref[...] = (c_ref[...].astype(F32) + d_ref[...].astype(F32)).astype(BF16)


def add_parts(right, forth, left, back):
    first = pl.BlockSpec((1, 256, 256), lambda i: (i, 0, 0))
    second = pl.BlockSpec((1, 256, 256), lambda i: (i + 4, 0, 0))
    out = jax.ShapeDtypeStruct((8, 256, 256), BF16)
    return pl.pallas_call(
        add_kernel,
        out_shape=(out, out),
        grid=(4,),
        in_specs=[first, first, second, first],
        out_specs=(first, second),
        input_output_aliases={0: 0, 2: 1},
        compiler_params=params(),
        cost_estimate=COST,
    )(right, forth, left, back)


def weight_grad_kernel(half_ref, r0, r1, theirs, g_ref, h_ref, out_ref):
    for k in range(4):
        columns = pl.ds(pl.multiple_of((half_ref[0] * 4 + k) * 256, 256), 256)
        total = None
        for t, g in (
            (r0[:, columns], g_ref[0]),
            (r1[:, columns], h_ref[0]),
            (theirs[:, 0, :, columns].reshape(256, 256), g_ref[1]),
            (theirs[:, 1, :, columns].reshape(256, 256), h_ref[1]),
        ):
            term = lax.dot_general(t, g, (((0,), (0,)), ((), ())), preferred_element_type=F32)
            total = term if total is None else total + term
        out_ref[k * 256 : k * 256 + 256] = (total * (1.0 / 64.0)).astype(BF16)


def weight_grad(half, *args):
    return pl.pallas_call(
        weight_grad_kernel,
        out_shape=jax.ShapeDtypeStruct((1024, 896), BF16),
        in_specs=[SMEM] + [VMEM] * 5,
        out_specs=VMEM,
        compiler_params=params(),
        cost_estimate=COST,
    )(half, *args)


def sum_over_x(d):
    return lax.psum_scatter(d, "dp", scatter_dimension=0, axis_index_groups=X_GROUPS, tiled=True)


def adam_kernel(opt_ref, *refs):
    mine_ref, recv_ref, hidden_ref, theirs_ref, master_ref, m_ref, v_ref = refs[:7]
    master_out, m_out, v_out, hidden_out = refs[7:]
    first = opt_ref[0] == 0
    low = low_lanes((recv_ref.shape[0], 128))
    fix_one = 1.0 - 0.9**20.0
    fix_two = 1.0 - 0.95**20.0

    def pick(half, mine, recv):
        return jnp.where(first, mine, recv) if half == 0 else jnp.where(first, recv, mine)

    def tile(half, at):
        return pick(half, mine_ref[:, at : at + 128].astype(F32), recv_ref[:, at : at + 128].astype(F32))

    def hidden_tile(half, at):
        recv = theirs_ref[:, at : at + 128].astype(F32)
        return pick(half, hidden_ref[:, at : at + 128].astype(F32), recv)

    mixed0, mixed1 = tile(0, 768), tile(1, 768)
    for j in range(14):
        part, k = divmod(j, 7)
        if k < 3:
            grads = tile(0, part * 384 + k * 128)
        elif k > 3:
            grads = tile(1, part * 384 + (k - 4) * 128)
        elif part == 0:
            grads = jnp.where(low, mixed0, pltpu.roll(mixed1, 64, 1))
        else:
            grads = jnp.where(low, pltpu.roll(mixed0, 64, 1), mixed1)
        at = slice(j * 128, j * 128 + 128)
        master = master_ref[:, at]
        one = 0.9 * m_ref[:, at].astype(F32) + 0.1 * grads
        two = 0.95 * v_ref[:, at].astype(F32) + 0.05 * grads * grads
        direction = one / fix_one / (jnp.sqrt(two / fix_two) + 1e-08)
        master_out[:, at] = master - 0.001 * (direction + 0.1 * master)
        m_out[:, at] = one.astype(BF16)
        v_out[:, at] = two.astype(BF16)
    for k in range(7):
        if k < 3:
            hidden = hidden_tile(0, k * 128)
        elif k > 3:
            hidden = hidden_tile(1, (k - 4) * 128)
        else:
            hidden = jnp.where(low, hidden_tile(0, 384), pltpu.roll(hidden_tile(1, 384), 64, 1))
        hidden_out[:, k * 128 : k * 128 + 128] = hidden.astype(BF16)


def adam(opt, *args):
    def rows(width):
        return pl.BlockSpec((32, width), lambda i, opt: (i, 0))

    return pl.pallas_call(
        adam_kernel,
        out_shape=(
            jax.ShapeDtypeStruct((256, 1792), F32),
            jax.ShapeDtypeStruct((256, 1792), BF16),
            jax.ShapeDtypeStruct((256, 1792), BF16),
            jax.ShapeDtypeStruct((256, 896), BF16),
        ),
        grid_spec=pltpu.PrefetchScalarGridSpec(
            num_scalar_prefetch=1,
            grid=(8,),
            in_specs=[rows(896)] * 2 + [rows(512)] * 2 + [rows(1792)] * 3,
            out_specs=(rows(1792), rows(1792), rows(1792), rows(896)),
        ),
        compiler_params=params(60 * 1024 * 1024),
        cost_estimate=COST,
    )(opt, *args)


def gather_x(block):
    return [block, along_x(block, 1), along_x(block, -1), along_x(block, 2)]


def body(tokens, grad_hidden, weight_codes, scales, master, first_moment, second_moment):
    o = lax.axis_index("opt")
    dp = lax.axis_index("dp")
    t = lax.axis_index("tensor")
    x, c = dp // 2, dp % 2
    zl, y = t // 4, t % 4
    z = o * 4 + zl
    opt = o.astype(jnp.int32).reshape(1)
    core = c.astype(jnp.int32).reshape(1)
    barrier = lax.optimization_barrier

    eighth = other_opt(lax.dynamic_slice_in_dim(tokens, (t % 8) * 32, 32, axis=0))
    r0, send = split_tokens(core, tokens)
    w_own, w_send = prepare(opt, scales, weight_codes)
    eighth, r0, send, w_own, w_send = barrier((eighth, r0, send, w_own, w_send))
    r1 = other_core(send)
    keep, part = split_tokens(core, eighth)
    theirs = lax.all_gather(jnp.stack([keep, other_core(part)]), "tensor", axis_index_groups=EIGHTHS)

    *near, w_recv = barrier((*gather_x(w_own), other_opt(w_send)))
    far = gather_x(w_recv)

    lower = grad_hidden[:, :512]
    upper = jnp.concatenate([grad_hidden[:, 512:], grad_hidden[:, 448:512], grad_hidden[:, 384:448]], axis=1)
    up_own = jnp.where(o == 0, lower, upper)
    up_send, _ = barrier((jnp.where(o == 0, upper, lower), w_recv))
    up_far = other_opt(up_send)

    xs = jnp.stack([x, (x + 3) % 4, (x + 1) % 4, (x + 2) % 4])
    at_near = (o * 4 + xs).astype(jnp.int32)
    at_far = ((1 - o) * 4 + xs).astype(jnp.int32)
    total, w_near = project_near(at_near, r0, r1, near)
    total, up_far, *far = barrier((total, up_far, *far))
    own, send, w_far = project_far(jnp.concatenate([at_near, at_far]), r0, r1, theirs, total, w_near, *far)
    recv, w_near_other = barrier((other_core(send), other_core(w_near)))
    hidden0, hidden1, g = swiglu(own, recv, up_own, up_far)
    g, w_far_other = barrier((g, other_core(w_far)))
    g_other = other_core(g)
    weights = [w_near, w_far, w_near_other, w_far_other]

    def table(*targets):
        which, block, half = [], [], []
        for ky, kz in targets:
            yt, zt = (y + ky) % 4, (z + kz) % 8
            zlt = zt % 4
            d = ((zlt % 2) * 2 + yt // 2 - x) % 4
            which.append(jnp.where(yt % 2 == c, 0, 2) + jnp.where(zlt // 2 == o, 0, 1))
            block.append(jnp.where(d == 0, 0, jnp.where(d == 3, 1, jnp.where(d == 1, 2, 3))))
            half.append(jnp.where(zt // 4 == o, 0, 1))
        return [jnp.stack(v).astype(jnp.int32) for v in (which, block, half)]

    def targets(*kys):
        return [(ky, kz) for ky in kys for kz in range(8)]

    forth, back = token_grad(table(*targets(2)), g, weights, 2)
    g, g_other, _ = barrier((g, g_other, forth))
    forth, back = along_y(forth, 1), along_y(back, -1)
    dw_far = weight_grad(1 - opt, r0, r1, theirs, g, g_other)
    g, g_other, _ = barrier((g, g_other, dw_far))
    right, left, mine = token_grad(table(*targets(1, 3, 0)), g, weights, 3)
    hidden_recv = other_opt(hidden1)
    forth, back, right, left, g, hidden_recv = barrier((forth, back, right, left, g, hidden_recv))
    right, left = add_parts(right, forth, left, back)
    right, left = along_y(right, 1), along_y(left, -1)
    dw_own = weight_grad(opt, r0, r1, theirs, g, g_other)
    dw_far, dw_own = sum_over_x(dw_far), sum_over_x(dw_own)
    right, left, mine, dw_recv = barrier((right, left, mine, other_opt(dw_far)))

    def piece(kz):
        return sum(a[kz].astype(F32) for a in (mine, right, left))

    up = along_z(piece(4).astype(BF16), 1)
    down = along_z(piece(5).astype(BF16), -1)
    updated = adam(opt, dw_own, dw_recv, hidden0, hidden_recv, master, first_moment, second_moment)
    up, down, *updated = barrier((up, down, *updated))
    up = along_z((up.astype(F32) + piece(3)).astype(BF16), 1)
    down = along_z((down.astype(F32) + piece(6)).astype(BF16), -1)
    up = along_z((up.astype(F32) + piece(2)).astype(BF16), 1)
    down = along_z((down.astype(F32) + piece(7)).astype(BF16), -1)
    up = along_z((up.astype(F32) + piece(1)).astype(BF16), 1)
    grad_tokens = (piece(0) + up.astype(F32) + down.astype(F32)).astype(BF16)
    new_master, new_first, new_second, hidden = updated
    return hidden, grad_tokens, new_master, new_first, new_second


def solution(mesh):
    rows = ("opt", "dp")
    in_specs = (
        P(rows, None),
        P(rows, "tensor"),
        P(rows, None, "tensor"),
        P(rows, "tensor"),
        P(rows, "tensor"),
        P(rows, "tensor"),
        P(rows, "tensor"),
    )
    out_specs = (P(rows, "tensor"),) * 5
    return jax.shard_map(body, mesh=mesh, in_specs=in_specs, out_specs=out_specs, check_vma=False)
```

time: 293 us -> 229 us (0.78)
  starting transfers between devices: 88.3 us -> 57.4 us
  waiting for transfers between devices: 93.6 us -> 68.1 us
  other arithmetic: 12.3 us -> 8.56 us
    ppermute x5, waiting for transfers between devices: 44.6 us -> 26.2 us  [other_opt(): return lax.ppermute(a, 'opt', [(0, 1), (1, 0)])]
    ppermute x5, starting transfers between devices: 39.8 us -> 26 us  [other_opt(): return lax.ppermute(a, 'opt', [(0, 1), (1, 0)])]
    ppermute x7, starting transfers between devices: 25.3 us -> 14.4 us  [along_z(): lax.ppermute(a, OT, [(z * 4 + y, (z + step) % 8 * 4 + y) for z in range(8...]
    unnamed x65 -> x56, local copies, waits for them, and re-layouts: 15.9 us -> 24.2 us
    ppermute x4, starting transfers between devices: 13.5 us -> 6.59 us  [along_y(): lax.ppermute(a, 'tensor', [(z * 4 + y, z * 4 + (y + step) % 4) for z in r...]
    slice x7 -> x0, local copies, waits for them, and re-layouts: 5.8 us -> none  [the longest x4 4.85 us: ring_gather(): far0, far1 = (along_x(before[:128], 1), along_x(after[128:], -1))]
    ppermute x7 -> x6, waiting for transfers between devices: 9.34 us -> 4.62 us  [other_core(): return lax.ppermute(a, 'dp', [(i, i ^ 1) for i in range(8)])]
    ppermute x7, waiting for transfers between devices: 5.76 us -> 10.1 us  [along_z(): lax.ppermute(a, OT, [(z * 4 + y, (z + step) % 8 * 4 + y) for z in range(8...]
  transfers between devices with their start and end apart: 34 -> 31, of which waited for: 18 -> 13; matrix products, arithmetic and copies ran while one was open for 11% -> 2% of each run, Pallas kernels for 13% -> 20%
where the time goes in v2:
time: 229 us; the launch traced here: 225 us
  waiting for transfers between devices  68.1 us (30%)
  starting transfers between devices  57.4 us (25%)
  Pallas kernels  49.3 us (22%)
  local copies, waits for them, and re-layouts  27.7 us (12%)
  between operations  14.4 us (6%)
  other arithmetic  8.56 us (4%)
    ppermute x5, waiting for transfers between devices, other_opt(): return lax.ppermute(a, 'opt', [(0, 1), (1, 0)])  26.2 us
    ppermute x5, starting transfers between devices, other_opt(): return lax.ppermute(a, 'opt', [(0, 1), (1, 0)])  26 us
    unnamed x56, local copies, waits for them, and re-layouts  24.2 us
    ppermute x4, waiting for transfers between devices, along_y(): lax.ppermute(a, 'tensor', [(z * 4 + y, z * 4 + (y + step) % 4) for z in r...  21.5 us
    pallas_call x2, Pallas kernels, token_grad(): pl.pallas_call(token_grad_kernel, out_shape=[jax.ShapeDtypeStruct((size,...  17.7 us
    ppermute x7, starting transfers between devices, along_z(): lax.ppermute(a, OT, [(z * 4 + y, (z + step) % 8 * 4 + y) for z in range(8...  14.4 us
    ppermute x7, waiting for transfers between devices, along_z(): lax.ppermute(a, OT, [(z * 4 + y, (z + step) % 8 * 4 + y) for z in range(8...  10.1 us
    ppermute x6, starting transfers between devices, along_x(): lax.ppermute(a, 'dp', [(x * 2 + c, (x + step) % 4 * 2 + c) for x in range...  9.35 us
  transfers between devices with their start and end apart: 31, of which 13 were waited for; matrix products, arithmetic and copies ran while one was open for 2% of the time, Pallas kernels for 20%

profile of v2, /device:TPU:14, one launch (start us, length us, event | category | flops | bytes accessed | tf_op | source)
XLA Modules:
  0.0 225.5 jit_solution(2740212974849976618)
XLA Ops:
  7.2 1.0 constant_dynamic-slice_fusion
  8.2 7.3 %collective-permute-start = (bf16[32,4096]{1,0:T(8,128)(2,1)S(1)}, bf16[32,4096]{1,0:T(8,128)(2,1)S(1)}, u32[]{:S(2)}, u32[]{:S(2)}) collective-permute-start(bf16[32,4096]{1,0:T(8,128)(2,1)S(1)} %constant_dynamic-slice_fusion), channel_id=1, source_target_pairs={{0,128},{128,0},{1,129},{129,1},{2,130},{130,2},{3,131},{131,3},{4... | collective-permute-start | bytes 786440 | tf_op jit(solution)/shard_map/ppermute | solution.py:32
  15.5 1.6 copy-done.5
  17.1 0.9 shard_map.110
  18.0 1.0 copy-done.23
  19.8 3.1 %collective-permute-done.keep_in.send_in = bf16[32,4096]{1,0:T(8,128)(2,1)S(1)} collective-permute-done((bf16[32,4096]{1,0:T(8,128)(2,1)S(1)}, bf16[32,4096]{1,0:T(8,128)(2,1)S(1)}, u32[]{:S(2)}, u32[]{:S(2)}) %collective-permute-start) | collective-permute-done | bytes 262176 | tf_op jit(solution)/shard_map/ppermute | solution.py:32
  23.4 1.3 collective-permute-done.2
  25.5 9.6 %collective-permute-start.6 = (bf16[256,896]{1,0:T(8,128)(2,1)S(1)}, bf16[256,896]{1,0:T(8,128)(2,1)S(1)}, u32[]{:S(2)}, u32[]{:S(2)}) collective-permute-start(bf16[256,896]{1,0:T(8,128)(2,1)S(1)} %get-tuple-element.81), channel_id=1, source_target_pairs={{0,128},{128,0},{1,129},{129,1},{2,130},{130,2},{3,131},{131,3},{4... | collective-permute-start | bytes 1376264 | tf_op jit(solution)/shard_map/ppermute | solution.py:32
  35.1 1.4 collective-permute-start.5
  36.5 3.2 %collective-permute-start.3 = (bf16[256,896]{1,0:T(8,128)(2,1)S(1)}, bf16[256,896]{1,0:T(8,128)(2,1)}, u32[]{:S(2)}, u32[]{:S(2)}) collective-permute-start(bf16[256,896]{1,0:T(8,128)(2,1)S(1)} %get-tuple-element.82.refs_0_), channel_id=1, source_target_pairs={{0,32},{16,48},{32,64},{48,80},{64,96},{80,112},{96,0},{112,16},{1... | collective-permute-start | bytes 1376264 | tf_op jit(solution)/shard_map/ppermute | solution.py:24
  39.7 0.9 slice.84
  40.7 1.0 fusion.9
  41.7 13.3 %collective-permute-done.6.refs_0_ = bf16[256,896]{1,0:T(8,128)(2,1)S(1)} collective-permute-done((bf16[256,896]{1,0:T(8,128)(2,1)S(1)}, bf16[256,896]{1,0:T(8,128)(2,1)S(1)}, u32[]{:S(2)}, u32[]{:S(2)}) %collective-permute-start.6) | collective-permute-done | bytes 458784 | tf_op jit(solution)/shard_map/ppermute | solution.py:32
  55.1 3.8 %collective-permute-done.4.refs_2_ = bf16[256,896]{1,0:T(8,128)(2,1)} collective-permute-done((bf16[256,896]{1,0:T(8,128)(2,1)S(1)}, bf16[256,896]{1,0:T(8,128)(2,1)}, u32[]{:S(2)}, u32[]{:S(2)}) %collective-permute-start.4) | collective-permute-done | bytes 458784 | tf_op jit(solution)/shard_map/ppermute | solution.py:24
  58.8 1.5 collective-permute-start.10
  60.3 3.2 %collective-permute-start.8 = (bf16[256,896]{1,0:T(8,128)(2,1)S(1)}, bf16[256,896]{1,0:T(8,128)(2,1)}, u32[]{:S(2)}, u32[]{:S(2)}) collective-permute-start(bf16[256,896]{1,0:T(8,128)(2,1)S(1)} %collective-permute-done.6.refs_0_), channel_id=1, source_target_pairs={{0,32},{16,48},{32,64},{48,80},{64,96},{80,112},{96,0},{112,16},{1... | collective-permute-start | bytes 1376264 | tf_op jit(solution)/shard_map/ppermute | solution.py:24
  63.6 1.8 broadcast_select_fusion
  65.4 2.6 %collective-permute-start.7 = (bf16[256,512]{1,0:T(8,128)(2,1)}, bf16[256,512]{1,0:T(8,128)(2,1)S(1)}, u32[]{:S(2)}, u32[]{:S(2)}) collective-permute-start(bf16[256,512]{1,0:T(8,128)(2,1)} %get-tuple-element.88), channel_id=1, source_target_pairs={{0,128},{128,0},{1,129},{129,1},{2,130},{130,2},{3,131},{131,3},{4... | collective-permute-start | bytes 786440 | tf_op jit(solution)/shard_map/ppermute | solution.py:32
  68.1 3.4 %shard_map.113 = (f32[512,896]{1,0:T(8,128)S(1)}, bf16[4,256,896]{2,1,0:T(8,128)(2,1)}) custom-call(s32[4]{0:T(128)S(1)} %get-tuple-element.137.at_ref, bf16[256,2048]{1,0:T(8,128)(2,1)S(1)} %get-tuple-element.75.r0_ref.r0, bf16[256,2048]{1,0:T(8,128)(2,1)S(1)} %collective-permute-done.1.r1_ref.r1, bf16[256,896]{1,0:T(8,128)(2,1)S(1)} %get-tuple-element.82.refs_0_, ...), custom_call_target="tpu_custom_call" | custom-call | flops 1 | bytes 1048576 | tf_op jit(solution)/shard_map/pallas_call | solution.py:133
  71.5 1.3 copy-done.14
  72.8 9.7 %collective-permute-done.7.refs_3_ = bf16[256,512]{1,0:T(8,128)(2,1)S(1)} collective-permute-done((bf16[256,512]{1,0:T(8,128)(2,1)}, bf16[256,512]{1,0:T(8,128)(2,1)S(1)}, u32[]{:S(2)}, u32[]{:S(2)}) %collective-permute-start.7) | collective-permute-done | bytes 262176 | tf_op jit(solution)/shard_map/ppermute | solution.py:32
  82.8 1.6 all-gather.3.cloned.1.call-done
  84.5 1.6 copy-done
  86.1 1.5 copy-done.15
  87.6 5.3 %shard_map.114 = (f32[2,256,896]{2,1,0:T(8,128)S(1)}, bf16[2,256,896]{2,1,0:T(8,128)(2,1)S(1)}, bf16[4,256,896]{2,1,0:T(8,128)(2,1)S(1)}) custom-call(s32[8]{0:T(128)S(1)} %pad_add_fusion.1.at_ref, bf16[256,2048]{1,0:T(8,128)(2,1)S(1)} %get-tuple-element.75.r0_ref.r0, bf16[256,2048]{1,0:T(8,128)(2,1)S(1)} %collective-permute-done.1.r1_ref.r1, ...), custom_call_target="tpu_custom_call" | custom-call | flops 1 | bytes 1048576 | tf_op jit(solution)/shard_map/pallas_call | solution.py:164
  93.0 1.3 copy-done.6
  94.8 3.3 %collective-permute-done.11.refs_1_ = bf16[2,256,896]{2,1,0:T(8,128)(2,1)S(1)} collective-permute-done((bf16[2,256,896]{2,1,0:T(8,128)(2,1)S(1)}, bf16[2,256,896]{2,1,0:T(8,128)(2,1)S(1)}, u32[]{:S(2)}, u32[]{:S(2)}) %collective-permute-start.11) | collective-permute-done | bytes 917536 | tf_op jit(solution)/shard_map/ppermute | solution.py:28
  98.1 1.9 shard_map.115
  101.4 1.3 copy-done.9
  103.1 1.5 copy-done.7
  104.6 1.5 copy-done.10
  106.1 5.4 %shard_map.116 = (bf16[4,256,256]{2,1,0:T(8,128)(2,1)S(1)}, bf16[4,256,256]{2,1,0:T(8,128)(2,1)S(1)}) custom-call(s32[8]{0:T(128)S(1)} %stack.290.which_ref, s32[8]{0:T(128)S(1)} %stack.299.block_ref, s32[8]{0:T(128)S(1)} %stack.308.half_ref, bf16[2,256,896]{2,1,0:T(8,128)(2,1)} %get-tuple-element.122.g_ref, ...), custom_call_target="tpu_custom_call" | custom-call | flops 1 | bytes 1048576 | tf_op jit(solution)/shard_map/pallas_call | solution.py:244
  113.1 3.8 %shard_map.117 = bf16[1024,896]{1,0:T(8,128)(2,1)S(1)} custom-call(s32[1]{0:T(128)S(6)} %sub.300.half_ref, bf16[256,2048]{1,0:T(8,128)(2,1)S(1)} %get-tuple-element.75.r0_ref.r0, bf16[256,2048]{1,0:T(8,128)(2,1)S(1)} %copy-done.3, bf16[8,2,32,2048]{3,2,1,0:T(8,128)(2,1)S(1)} %bitcast.112, bf16[2,256,896]{2,1,0:T(8,128)(2,1)} %get-tuple-element.122.g_ref, ...), custom_call_target="tpu_custom_call" | custom-call | flops 1 | bytes 1048576 | tf_op jit(solution)/shard_map/pallas_call | solution.py:291
  117.0 1.3 copy-done.12
  118.3 2.4 %collective-permute-start.15 = (bf16[4,256,256]{2,1,0:T(8,128)(2,1)}, bf16[4,256,256]{2,1,0:T(8,128)(2,1)}, u32[]{:S(2)}, u32[]{:S(2)}) collective-permute-start(bf16[4,256,256]{2,1,0:T(8,128)(2,1)} %copy-done.25), channel_id=1, source_target_pairs={{0,3},{1,0},{2,1},{3,2},{4,7},{5,4},{6,5},{7,6},{8,11},{9,8},{10,9... | collective-permute-start | bytes 1572872 | tf_op jit(solution)/shard_map/ppermute | solution.py:36
  120.8 1.5 collective-permute-start.14
  122.3 2.6 %collective-permute-start.17 = (bf16[256,512]{1,0:T(8,128)(2,1)S(1)}, bf16[256,512]{1,0:T(8,128)(2,1)}, u32[]{:S(2)}, u32[]{:S(2)}) collective-permute-start(bf16[256,512]{1,0:T(8,128)(2,1)S(1)} %copy-done.27), channel_id=1, source_target_pairs={{0,128},{128,0},{1,129},{129,1},{2,130},{130,2},{3,131},{131,3},{4... | collective-permute-start | bytes 786440 | tf_op jit(solution)/shard_map/ppermute | solution.py:32
  125.7 1.5 copy-done.8
  127.2 1.5 copy-done.11
  128.7 12.3 %shard_map.118 = (bf16[8,256,256]{2,1,0:T(8,128)(2,1)S(1)}, bf16[8,256,256]{2,1,0:T(8,128)(2,1)}, bf16[8,256,256]{2,1,0:T(8,128)(2,1)S(1)}) custom-call(s32[24]{0:T(128)S(1)} %stack.341.which_ref, s32[24]{0:T(128)S(1)} %stack.366.block_ref, s32[24]{0:T(128)S(1)} %stack.367.half_ref, bf16[2,256,896]{2,1,0:T(8,128)(2,1)} %get-tuple-element.122.g_ref, ...), custom_call_target="tpu_custom_call" | custom-call | flops 1 | bytes 1048576 | tf_op jit(solution)/shard_map/pallas_call | solution.py:244
  141.0 1.0 copy-done.16
  141.9 1.0 copy-done.18
  142.9 3.9 %shard_map.120 = bf16[1024,896]{1,0:T(8,128)(2,1)S(1)} custom-call(s32[1]{0:T(128)} %bitcast.29.opt_ref.half_ref, bf16[256,2048]{1,0:T(8,128)(2,1)S(1)} %get-tuple-element.75.r0_ref.r0, bf16[256,2048]{1,0:T(8,128)(2,1)S(1)} %copy-done.4, bf16[8,2,32,2048]{3,2,1,0:T(8,128)(2,1)S(1)} %bitcast.113, bf16[2,256,896]{2,1,0:T(8,128)(2,1)} %get-tuple-element.122.g_ref, ...), custom_call_target="tpu_custom_call" | custom-call | flops 1 | bytes 1048576 | tf_op jit(solution)/shard_map/pallas_call | solution.py:291
  146.8 1.2 copy-done.13
  148.0 1.2 copy-done.17
  149.2 3.5 %shard_map.119 = (bf16[8,256,256]{2,1,0:T(8,128)(2,1)S(1)}, bf16[8,256,256]{2,1,0:T(8,128)(2,1)}) custom-call(bf16[8,256,256]{2,1,0:T(8,128)(2,1)S(1)} %copy-done.17, bf16[4,256,256]{2,1,0:T(8,128)(2,1)} %collective-permute-done.14.b_ref, bf16[8,256,256]{2,1,0:T(8,128)(2,1)} %get-tuple-element.114.c_ref, ...), custom_call_target="tpu_custom_call", output_to_operand_aliasing={{0}: (0, {}), {1}: (2, {})} | custom-call | flops 1 | bytes 1048576 | tf_op jit(solution)/shard_map/pallas_call | solution.py:263
  152.8 2.2 collective-permute-start.18
  155.4 3.9 %collective-permute-start.20 = (bf16[256,896]{1,0:T(8,128)(2,1)}, bf16[256,896]{1,0:T(8,128)(2,1)}, u32[]{:S(2)}, u32[]{:S(2)}) collective-permute-start(bf16[256,896]{1,0:T(8,128)(2,1)} %reduce-scatter.3.cloned.1.call-done), channel_id=1, source_target_pairs={{0,128},{128,0},{1,129},{129,1},{2,130},{130,2},{3,131},{131,3},{4... | collective-permute-start | bytes 1376264 | tf_op jit(solution)/shard_map/ppermute | solution.py:32
  159.4 19.2 %collective-permute-done.18 = bf16[8,256,256]{2,1,0:T(8,128)(2,1)S(1)} collective-permute-done((bf16[8,256,256]{2,1,0:T(8,128)(2,1)S(1)}, bf16[8,256,256]{2,1,0:T(8,128)(2,1)S(1)}, u32[]{:S(2)}, u32[]{:S(2)}) %collective-permute-start.18) | collective-permute-done | bytes 1048608 | tf_op jit(solution)/shard_map/ppermute | solution.py:36
  178.5 2.4 %collective-permute-done.19 = bf16[8,256,256]{2,1,0:T(8,128)(2,1)} collective-permute-done((bf16[8,256,256]{2,1,0:T(8,128)(2,1)}, bf16[8,256,256]{2,1,0:T(8,128)(2,1)}, u32[]{:S(2)}, u32[]{:S(2)}) %collective-permute-start.19) | collective-permute-done | bytes 1048608 | tf_op jit(solution)/shard_map/ppermute | solution.py:36
  180.9 1.1 fusion.8
  182.0 2.3 %collective-permute-start.22 = (bf16[256,256]{1,0:T(8,128)(2,1)S(1)}, bf16[256,256]{1,0:T(8,128)(2,1)S(1)}, u32[]{:S(2)}, u32[]{:S(2)}) collective-permute-start(bf16[256,256]{1,0:T(8,128)(2,1)S(1)} %get-tuple-element.143), channel_id=1, source_target_pairs={{0,140},{1,141},{2,142},{3,143},{4,0},{5,1},{6,2},{7,3},{8,4},{9,5... | collective-permute-start | bytes 393224 | tf_op jit(solution)/shard_map/ppermute | solution.py:40
  184.3 3.4 %collective-permute-start.21 = (bf16[256,256]{1,0:T(8,128)(2,1)S(1)}, bf16[256,256]{1,0:T(8,128)(2,1)S(1)}, u32[]{:S(2)}, u32[]{:S(2)}) collective-permute-start(bf16[256,256]{1,0:T(8,128)(2,1)S(1)} %get-tuple-element.144), channel_id=1, source_target_pairs={{0,4},{1,5},{2,6},{3,7},{4,8},{5,9},{6,10},{7,11},{8,12},{9,13},{1... | collective-permute-start | bytes 393224 | tf_op jit(solution)/shard_map/ppermute | solution.py:40
  187.6 7.7 %shard_map.121 = (f32[256,1792]{1,0:T(8,128)}, bf16[256,1792]{1,0:T(8,128)(2,1)}, bf16[256,1792]{1,0:T(8,128)(2,1)}, bf16[256,896]{1,0:T(8,128)(2,1)}) custom-call(s32[1]{0:T(128)} %bitcast.29.opt_ref.half_ref, bf16[256,896]{1,0:T(8,128)(2,1)} %reduce-scatter.5.cloned.1.call-done.refs_0_, bf16[256,896]{1,0:T(8,128)(2,1)} %collective-permute-done.20.refs_1_, ...), custom_call_target="tpu_custom_call" | custom-call | flops 1 | bytes 1048576 | tf_op jit(solution)/shard_map/pallas_call | solution.py:356
  195.3 1.0 fusion.4
  196.3 2.0 collective-permute-start.23
  198.3 4.2 %collective-permute-done.23 = bf16[256,256]{1,0:T(8,128)(2,1)S(1)} collective-permute-done((bf16[256,256]{1,0:T(8,128)(2,1)S(1)}, bf16[256,256]{1,0:T(8,128)(2,1)S(1)}, u32[]{:S(2)}, u32[]{:S(2)}) %collective-permute-start.23) | collective-permute-done | bytes 131104 | tf_op jit(solution)/shard_map/ppermute | solution.py:40
  202.5 1.1 fusion.3
  204.4 2.5 %collective-permute-start.26 = (bf16[256,256]{1,0:T(8,128)(2,1)S(1)}, bf16[256,256]{1,0:T(8,128)(2,1)S(1)}, u32[]{:S(2)}, u32[]{:S(2)}) collective-permute-start(bf16[256,256]{1,0:T(8,128)(2,1)S(1)} %get-tuple-element.142), channel_id=1, source_target_pairs={{0,140},{1,141},{2,142},{3,143},{4,0},{5,1},{6,2},{7,3},{8,4},{9,5... | collective-permute-start | bytes 393224 | tf_op jit(solution)/shard_map/ppermute | solution.py:40
  207.0 2.9 %collective-permute-done.24 = bf16[256,256]{1,0:T(8,128)(2,1)S(1)} collective-permute-done((bf16[256,256]{1,0:T(8,128)(2,1)S(1)}, bf16[256,256]{1,0:T(8,128)(2,1)S(1)}, u32[]{:S(2)}, u32[]{:S(2)}) %collective-permute-start.24) | collective-permute-done | bytes 131104 | tf_op jit(solution)/shard_map/ppermute | solution.py:40
  209.9 1.1 fusion.2
  211.9 2.5 %collective-permute-start.27 = (bf16[256,256]{1,0:T(8,128)(2,1)S(1)}, bf16[256,256]{1,0:T(8,128)(2,1)S(1)}, u32[]{:S(2)}, u32[]{:S(2)}) collective-permute-start(bf16[256,256]{1,0:T(8,128)(2,1)S(1)} %get-tuple-element.140), channel_id=1, source_target_pairs={{0,140},{1,141},{2,142},{3,143},{4,0},{5,1},{6,2},{7,3},{8,4},{9,5... | collective-permute-start | bytes 393224 | tf_op jit(solution)/shard_map/ppermute | solution.py:40
  214.4 2.9 %collective-permute-done.25 = bf16[256,256]{1,0:T(8,128)(2,1)S(1)} collective-permute-done((bf16[256,256]{1,0:T(8,128)(2,1)S(1)}, bf16[256,256]{1,0:T(8,128)(2,1)S(1)}, u32[]{:S(2)}, u32[]{:S(2)}) %collective-permute-start.25) | collective-permute-done | bytes 131104 | tf_op jit(solution)/shard_map/ppermute | solution.py:40
  217.3 1.6 fusion.6
  (88 shorter events, 9.2 us)
Async XLA Ops:
  7.2 77.3 %all-gather.3.cloned.1.call-start = ((), (), s32[]{:S(2)}) async-start(), calls=%async_computation.4 | async-start | bytes 2359296 | tf_op jit(solution)/shard_map/all_gather | solution.py:396
  8.2 14.7 %collective-permute-start = (bf16[32,4096]{1,0:T(8,128)(2,1)S(1)}, bf16[32,4096]{1,0:T(8,128)(2,1)S(1)}, u32[]{:S(2)}, u32[]{:S(2)}) collective-permute-start(bf16[32,4096]{1,0:T(8,128)(2,1)S(1)} %constant_dynamic-slice_fusion), channel_id=1, source_target_pairs={{0,128},{128,0},{1,129},{129,1},{2,130},{130,2},{3,131},{131,3},{4... | collective-permute-start | bytes 786440 | tf_op jit(solution)/shard_map/ppermute | solution.py:32
  15.5 1.6 copy-start.5
  17.1 1.9 copy-start.20
  17.1 1.9 copy-start.22
  18.0 1.0 copy-start.23
  23.3 1.4 collective-permute-start.2
  25.5 130.0 %reduce-scatter.3.cloned.1.call-start = ((), (), s32[]{:S(2)}) async-start(), calls=%async_computation.2 | async-start | bytes 2293760 | tf_op jit(solution)/shard_map/reduce_scatter | solution.py:302
  25.5 29.5 %collective-permute-start.6 = (bf16[256,896]{1,0:T(8,128)(2,1)S(1)}, bf16[256,896]{1,0:T(8,128)(2,1)S(1)}, u32[]{:S(2)}, u32[]{:S(2)}) collective-permute-start(bf16[256,896]{1,0:T(8,128)(2,1)S(1)} %get-tuple-element.81), channel_id=1, source_target_pairs={{0,128},{128,0},{1,129},{129,1},{2,130},{130,2},{3,131},{131,3},{4... | collective-permute-start | bytes 1376264 | tf_op jit(solution)/shard_map/ppermute | solution.py:32
  35.1 20.0 %collective-permute-start.5 = (bf16[256,896]{1,0:T(8,128)(2,1)S(1)}, bf16[256,896]{1,0:T(8,128)(2,1)}, u32[]{:S(2)}, u32[]{:S(2)}) collective-permute-start(bf16[256,896]{1,0:T(8,128)(2,1)S(1)} %get-tuple-element.82.refs_0_), channel_id=1, source_target_pairs={{0,64},{16,80},{32,96},{48,112},{64,0},{80,16},{96,32},{112,48},{1... | collective-permute-start | bytes 1376264 | tf_op jit(solution)/shard_map/ppermute | solution.py:24
  36.5 22.3 %collective-permute-start.4 = (bf16[256,896]{1,0:T(8,128)(2,1)S(1)}, bf16[256,896]{1,0:T(8,128)(2,1)}, u32[]{:S(2)}, u32[]{:S(2)}) collective-permute-start(bf16[256,896]{1,0:T(8,128)(2,1)S(1)} %get-tuple-element.82.refs_0_), channel_id=1, source_target_pairs={{0,96},{16,112},{32,0},{48,16},{64,32},{80,48},{96,64},{112,80},{1... | collective-permute-start | bytes 1376264 | tf_op jit(solution)/shard_map/ppermute | solution.py:24
  36.5 22.3 %collective-permute-start.3 = (bf16[256,896]{1,0:T(8,128)(2,1)S(1)}, bf16[256,896]{1,0:T(8,128)(2,1)}, u32[]{:S(2)}, u32[]{:S(2)}) collective-permute-start(bf16[256,896]{1,0:T(8,128)(2,1)S(1)} %get-tuple-element.82.refs_0_), channel_id=1, source_target_pairs={{0,32},{16,48},{32,64},{48,80},{64,96},{80,112},{96,0},{112,16},{1... | collective-permute-start | bytes 1376264 | tf_op jit(solution)/shard_map/ppermute | solution.py:24
  39.7 28.4 %collective-permute-start.1 = (bf16[256,2048]{1,0:T(8,128)(2,1)}, bf16[256,2048]{1,0:T(8,128)(2,1)S(1)}, u32[]{:S(2)}, u32[]{:S(2)}) collective-permute-start(bf16[256,2048]{1,0:T(8,128)(2,1)} %copy-done.23), channel_id=1, source_target_pairs={{0,16},{16,0},{32,48},{48,32},{64,80},{80,64},{96,112},{112,96},{1... | collective-permute-start | bytes 3145736 | tf_op jit(solution)/shard_map/ppermute | solution.py:28
  58.8 23.7 %collective-permute-start.10 = (bf16[256,896]{1,0:T(8,128)(2,1)S(1)}, bf16[256,896]{1,0:T(8,128)(2,1)}, u32[]{:S(2)}, u32[]{:S(2)}) collective-permute-start(bf16[256,896]{1,0:T(8,128)(2,1)S(1)} %collective-permute-done.6.refs_0_), channel_id=1, source_target_pairs={{0,64},{16,80},{32,96},{48,112},{64,0},{80,16},{96,32},{112,48},{1... | collective-permute-start | bytes 1376264 | tf_op jit(solution)/shard_map/ppermute | solution.py:24
  60.3 22.4 %collective-permute-start.9 = (bf16[256,896]{1,0:T(8,128)(2,1)S(1)}, bf16[256,896]{1,0:T(8,128)(2,1)}, u32[]{:S(2)}, u32[]{:S(2)}) collective-permute-start(bf16[256,896]{1,0:T(8,128)(2,1)S(1)} %collective-permute-done.6.refs_0_), channel_id=1, source_target_pairs={{0,96},{16,112},{32,0},{48,16},{64,32},{80,48},{96,64},{112,80},{1... | collective-permute-start | bytes 1376264 | tf_op jit(solution)/shard_map/ppermute | solution.py:24
  60.3 22.4 %collective-permute-start.8 = (bf16[256,896]{1,0:T(8,128)(2,1)S(1)}, bf16[256,896]{1,0:T(8,128)(2,1)}, u32[]{:S(2)}, u32[]{:S(2)}) collective-permute-start(bf16[256,896]{1,0:T(8,128)(2,1)S(1)} %collective-permute-done.6.refs_0_), channel_id=1, source_target_pairs={{0,32},{16,48},{32,64},{48,80},{64,96},{80,112},{96,0},{112,16},{1... | collective-permute-start | bytes 1376264 | tf_op jit(solution)/shard_map/ppermute | solution.py:24
  65.4 17.1 %collective-permute-start.7 = (bf16[256,512]{1,0:T(8,128)(2,1)}, bf16[256,512]{1,0:T(8,128)(2,1)S(1)}, u32[]{:S(2)}, u32[]{:S(2)}) collective-permute-start(bf16[256,512]{1,0:T(8,128)(2,1)} %get-tuple-element.88), channel_id=1, source_target_pairs={{0,128},{128,0},{1,129},{129,1},{2,130},{130,2},{3,131},{131,3},{4... | collective-permute-start | bytes 786440 | tf_op jit(solution)/shard_map/ppermute | solution.py:32
  68.1 16.4 %copy-start.2 = (bf16[256,2048]{1,0:T(8,128)(2,1)}, bf16[256,2048]{1,0:T(8,128)(2,1)S(1)}, u32[]{:S(2)}) copy-start(bf16[256,2048]{1,0:T(8,128)(2,1)S(1)} %collective-permute-done.1.r1_ref.r1) | copy-start | bytes 3145732
  71.5 1.3 copy-start.14
  82.7 12.1 %collective-permute-start.12 = (bf16[4,256,896]{2,1,0:T(8,128)(2,1)}, bf16[4,256,896]{2,1,0:T(8,128)(2,1)}, u32[]{:S(2)}, u32[]{:S(2)}) collective-permute-start(bf16[4,256,896]{2,1,0:T(8,128)(2,1)} %get-tuple-element.90.near_ref.refs_0_), channel_id=1, source_target_pairs={{0,16},{16,0},{32,48},{48,32},{64,80},{80,64},{96,112},{112,96},{1... | collective-permute-start | bytes 5505032 | tf_op jit(solution)/shard_map/ppermute | solution.py:28
  84.5 1.6 copy-start
  86.1 1.5 copy-start.15
  92.9 8.5 %collective-permute-start.13 = (bf16[4,256,896]{2,1,0:T(8,128)(2,1)S(1)}, bf16[4,256,896]{2,1,0:T(8,128)(2,1)S(1)}, u32[]{:S(2)}, u32[]{:S(2)}) collective-permute-start(bf16[4,256,896]{2,1,0:T(8,128)(2,1)S(1)} %get-tuple-element.100.refs_1_), channel_id=1, source_target_pairs={{0,16},{16,0},{32,48},{48,32},{64,80},{80,64},{96,112},{112,96},{1... | collective-permute-start | bytes 5505032 | tf_op jit(solution)/shard_map/ppermute | solution.py:28
  93.0 1.3 copy-start.6
  94.3 3.8 %collective-permute-start.11 = (bf16[2,256,896]{2,1,0:T(8,128)(2,1)S(1)}, bf16[2,256,896]{2,1,0:T(8,128)(2,1)S(1)}, u32[]{:S(2)}, u32[]{:S(2)}) collective-permute-start(bf16[2,256,896]{2,1,0:T(8,128)(2,1)S(1)} %get-tuple-element.96), channel_id=1, source_target_pairs={{0,16},{16,0},{32,48},{48,32},{64,80},{80,64},{96,112},{112,96},{1... | collective-permute-start | bytes 2752520 | tf_op jit(solution)/shard_map/ppermute | solution.py:28
  100.0 0.7 copy-start.21
  100.7 0.7 copy-start.26
  101.4 1.3 copy-start.9
  102.7 10.4 %collective-permute-start.16 = (bf16[2,256,896]{2,1,0:T(8,128)(2,1)}, bf16[2,256,896]{2,1,0:T(8,128)(2,1)}, u32[]{:S(2)}, u32[]{:S(2)}) collective-permute-start(bf16[2,256,896]{2,1,0:T(8,128)(2,1)} %get-tuple-element.122.g_ref), channel_id=1, source_target_pairs={{0,16},{16,0},{32,48},{48,32},{64,80},{80,64},{96,112},{112,96},{1... | collective-permute-start | bytes 2752520 | tf_op jit(solution)/shard_map/ppermute | solution.py:28
  103.1 1.5 copy-start.7
  104.6 1.5 copy-start.10
  106.1 7.0 %copy-start.1 = (bf16[16,32,2048]{2,1,0:T(8,128)(2,1)S(1)}, bf16[16,32,2048]{2,1,0:T(8,128)(2,1)}, u32[]{:S(2)}) copy-start(bf16[16,32,2048]{2,1,0:T(8,128)(2,1)} %all-gather.3.cloned.1.call-done) | copy-start | bytes 6291460
  106.1 7.0 %copy-start.3 = (bf16[256,2048]{1,0:T(8,128)(2,1)S(1)}, bf16[256,2048]{1,0:T(8,128)(2,1)}, u32[]{:S(2)}) copy-start(bf16[256,2048]{1,0:T(8,128)(2,1)} %copy-done.2) | copy-start | bytes 3145732
  111.5 0.8 copy-start.24
  112.3 0.8 copy-start.25
  117.0 1.3 copy-start.12
  118.3 4.0 %copy-start.27 = (bf16[256,512]{1,0:T(8,128)(2,1)S(1)}, bf16[256,512]{1,0:T(8,128)(2,1)}, u32[]{:S(2)}) copy-start(bf16[256,512]{1,0:T(8,128)(2,1)} %copy-done.26) | copy-start | bytes 786436
  118.3 69.3 %reduce-scatter.5.cloned.1.call-start = ((), (), s32[]{:S(2)}) async-start(), calls=%async_computation.3 | async-start | bytes 2293760 | tf_op jit(solution)/shard_map/reduce_scatter | solution.py:302
  118.3 24.6 %collective-permute-start.15 = (bf16[4,256,256]{2,1,0:T(8,128)(2,1)}, bf16[4,256,256]{2,1,0:T(8,128)(2,1)}, u32[]{:S(2)}, u32[]{:S(2)}) collective-permute-start(bf16[4,256,256]{2,1,0:T(8,128)(2,1)} %copy-done.25), channel_id=1, source_target_pairs={{0,3},{1,0},{2,1},{3,2},{4,7},{5,4},{6,5},{7,6},{8,11},{9,8},{10,9... | collective-permute-start | bytes 1572872 | tf_op jit(solution)/shard_map/ppermute | solution.py:36
  120.8 22.1 %collective-permute-start.14 = (bf16[4,256,256]{2,1,0:T(8,128)(2,1)}, bf16[4,256,256]{2,1,0:T(8,128)(2,1)}, u32[]{:S(2)}, u32[]{:S(2)}) collective-permute-start(bf16[4,256,256]{2,1,0:T(8,128)(2,1)} %copy-done.24), channel_id=1, source_target_pairs={{0,1},{1,2},{2,3},{3,0},{4,5},{5,6},{6,7},{7,4},{8,9},{9,10},{10,1... | collective-permute-start | bytes 1572872 | tf_op jit(solution)/shard_map/ppermute | solution.py:36
  122.3 20.6 %collective-permute-start.17 = (bf16[256,512]{1,0:T(8,128)(2,1)S(1)}, bf16[256,512]{1,0:T(8,128)(2,1)}, u32[]{:S(2)}, u32[]{:S(2)}) collective-permute-start(bf16[256,512]{1,0:T(8,128)(2,1)S(1)} %copy-done.27), channel_id=1, source_target_pairs={{0,128},{128,0},{1,129},{129,1},{2,130},{130,2},{3,131},{131,3},{4... | collective-permute-start | bytes 786440 | tf_op jit(solution)/shard_map/ppermute | solution.py:32
  125.7 1.5 copy-start.8
  127.2 1.5 copy-start.11
  128.7 14.3 %copy-start.4 = (bf16[256,2048]{1,0:T(8,128)(2,1)S(1)}, bf16[256,2048]{1,0:T(8,128)(2,1)}, u32[]{:S(2)}) copy-start(bf16[256,2048]{1,0:T(8,128)(2,1)} %copy-done.2) | copy-start | bytes 3145732
  141.0 1.0 copy-start.16
  141.9 1.0 copy-start.18
  146.8 1.2 copy-start.13
  148.0 1.2 copy-start.17
  149.2 31.7 %copy-start.19 = (bf16[8,256,256]{2,1,0:T(8,128)(2,1)S(1)}, bf16[8,256,256]{2,1,0:T(8,128)(2,1)}, u32[]{:S(2)}) copy-start(bf16[8,256,256]{2,1,0:T(8,128)(2,1)} %copy-done.18) | copy-start | bytes 3145732
  152.8 25.7 %collective-permute-start.18 = (bf16[8,256,256]{2,1,0:T(8,128)(2,1)S(1)}, bf16[8,256,256]{2,1,0:T(8,128)(2,1)S(1)}, u32[]{:S(2)}, u32[]{:S(2)}) collective-permute-start(bf16[8,256,256]{2,1,0:T(8,128)(2,1)S(1)} %get-tuple-element.116), channel_id=1, source_target_pairs={{0,1},{1,2},{2,3},{3,0},{4,5},{5,6},{6,7},{7,4},{8,9},{9,10},{10,1... | collective-permute-start | bytes 3145736 | tf_op jit(solution)/shard_map/ppermute | solution.py:36
  154.9 26.0 %collective-permute-start.19 = (bf16[8,256,256]{2,1,0:T(8,128)(2,1)}, bf16[8,256,256]{2,1,0:T(8,128)(2,1)}, u32[]{:S(2)}, u32[]{:S(2)}) collective-permute-start(bf16[8,256,256]{2,1,0:T(8,128)(2,1)} %get-tuple-element.117), channel_id=1, source_target_pairs={{0,3},{1,0},{2,1},{3,2},{4,7},{5,4},{6,5},{7,6},{8,11},{9,8},{10,9... | collective-permute-start | bytes 3145736 | tf_op jit(solution)/shard_map/ppermute | solution.py:36
  155.4 25.5 %collective-permute-start.20 = (bf16[256,896]{1,0:T(8,128)(2,1)}, bf16[256,896]{1,0:T(8,128)(2,1)}, u32[]{:S(2)}, u32[]{:S(2)}) collective-permute-start(bf16[256,896]{1,0:T(8,128)(2,1)} %reduce-scatter.3.cloned.1.call-done), channel_id=1, source_target_pairs={{0,128},{128,0},{1,129},{129,1},{2,130},{130,2},{3,131},{131,3},{4... | collective-permute-start | bytes 1376264 | tf_op jit(solution)/shard_map/ppermute | solution.py:32
  182.0 13.3 %collective-permute-start.22 = (bf16[256,256]{1,0:T(8,128)(2,1)S(1)}, bf16[256,256]{1,0:T(8,128)(2,1)S(1)}, u32[]{:S(2)}, u32[]{:S(2)}) collective-permute-start(bf16[256,256]{1,0:T(8,128)(2,1)S(1)} %get-tuple-element.143), channel_id=1, source_target_pairs={{0,140},{1,141},{2,142},{3,143},{4,0},{5,1},{6,2},{7,3},{8,4},{9,5... | collective-permute-start | bytes 393224 | tf_op jit(solution)/shard_map/ppermute | solution.py:40
  184.3 11.0 %collective-permute-start.21 = (bf16[256,256]{1,0:T(8,128)(2,1)S(1)}, bf16[256,256]{1,0:T(8,128)(2,1)S(1)}, u32[]{:S(2)}, u32[]{:S(2)}) collective-permute-start(bf16[256,256]{1,0:T(8,128)(2,1)S(1)} %get-tuple-element.144), channel_id=1, source_target_pairs={{0,4},{1,5},{2,6},{3,7},{4,8},{5,9},{6,10},{7,11},{8,12},{9,13},{1... | collective-permute-start | bytes 393224 | tf_op jit(solution)/shard_map/ppermute | solution.py:40
  196.3 6.3 %collective-permute-start.23 = (bf16[256,256]{1,0:T(8,128)(2,1)S(1)}, bf16[256,256]{1,0:T(8,128)(2,1)S(1)}, u32[]{:S(2)}, u32[]{:S(2)}) collective-permute-start(bf16[256,256]{1,0:T(8,128)(2,1)S(1)} %fusion.4), channel_id=1, source_target_pairs={{0,4},{1,5},{2,6},{3,7},{4,8},{5,9},{6,10},{7,11},{8,12},{9,13},{1... | collective-permute-start | bytes 393224 | tf_op jit(solution)/shard_map/ppermute | solution.py:40
  203.6 6.3 %collective-permute-start.24 = (bf16[256,256]{1,0:T(8,128)(2,1)S(1)}, bf16[256,256]{1,0:T(8,128)(2,1)S(1)}, u32[]{:S(2)}, u32[]{:S(2)}) collective-permute-start(bf16[256,256]{1,0:T(8,128)(2,1)S(1)} %get-tuple-element.141), channel_id=1, source_target_pairs={{0,4},{1,5},{2,6},{3,7},{4,8},{5,9},{6,10},{7,11},{8,12},{9,13},{1... | collective-permute-start | bytes 393224 | tf_op jit(solution)/shard_map/ppermute | solution.py:40
  204.4 5.5 %collective-permute-start.26 = (bf16[256,256]{1,0:T(8,128)(2,1)S(1)}, bf16[256,256]{1,0:T(8,128)(2,1)S(1)}, u32[]{:S(2)}, u32[]{:S(2)}) collective-permute-start(bf16[256,256]{1,0:T(8,128)(2,1)S(1)} %get-tuple-element.142), channel_id=1, source_target_pairs={{0,140},{1,141},{2,142},{3,143},{4,0},{5,1},{6,2},{7,3},{8,4},{9,5... | collective-permute-start | bytes 393224 | tf_op jit(solution)/shard_map/ppermute | solution.py:40
  211.0 6.3 %collective-permute-start.25 = (bf16[256,256]{1,0:T(8,128)(2,1)S(1)}, bf16[256,256]{1,0:T(8,128)(2,1)S(1)}, u32[]{:S(2)}, u32[]{:S(2)}) collective-permute-start(bf16[256,256]{1,0:T(8,128)(2,1)S(1)} %get-tuple-element.139), channel_id=1, source_target_pairs={{0,4},{1,5},{2,6},{3,7},{4,8},{5,9},{6,10},{7,11},{8,12},{9,13},{1... | collective-permute-start | bytes 393224 | tf_op jit(solution)/shard_map/ppermute | solution.py:40
  211.9 5.4 %collective-permute-start.27 = (bf16[256,256]{1,0:T(8,128)(2,1)S(1)}, bf16[256,256]{1,0:T(8,128)(2,1)S(1)}, u32[]{:S(2)}, u32[]{:S(2)}) collective-permute-start(bf16[256,256]{1,0:T(8,128)(2,1)S(1)} %get-tuple-element.140), channel_id=1, source_target_pairs={{0,140},{1,141},{2,142},{3,143},{4,0},{5,1},{6,2},{7,3},{8,4},{9,5... | collective-permute-start | bytes 393224 | tf_op jit(solution)/shard_map/ppermute | solution.py:40
Sparse Core Ops, SparseCore 0:
  25.6 58.8 all-gather.2
  118.4 34.2 reduce-scatter.2
  155.8 29.7 reduce-scatter.4
